TPU v7x, 256 devices: a whole 4x4x8 slice. The times are simulated.
256 devices in a mesh: lat: 4 (over x_lo, core), lon: 64 (over y, x_hi, z).
Axes of the slice: x: 4 (x_hi: 2, x_lo: 2; x = x_hi * 2 + x_lo), y: 4, z: 8, core: 2. Of those that a mesh axis runs over, the one named last changes fastest.
Arguments:
- fields: bfloat16 [512, 1024, 70], P('lat', 'lon'), may hold values from -6 to 6
- row_valid: int32 [512], P('lat'), may hold values from 0 to 1, as said below
- w_encode: bfloat16 [70, 1024], replicated, may hold values from -0.75 to 0.75
- norm_gain: float32 [1024], replicated, may hold values from 0.1 to 1.9
- w_query: bfloat16 [1024, 512], replicated, may hold values from -0.1875 to 0.1875
- w_key: bfloat16 [1024, 512], replicated, may hold values from -0.1875 to 0.1875
- w_value: bfloat16 [1024, 512], replicated, may hold values from -0.1875 to 0.1875
- query_gain: float32 [64], replicated, may hold values from 0.1 to 1.9
- key_gain: float32 [64], replicated, may hold values from 0.1 to 1.9
- w_out: bfloat16 [512, 1024], replicated, may hold values from -1 to 1
Outputs:
- layer_out: bfloat16 [512, 1024, 1024], P('lat', 'lon')
Inputs may be any that keep to these rules, and one draw needn't show every extreme that they name: `row_valid`: for one t of 1 to 6, the first t rows and the last 7 - t rows are 0 and all others are 1.
All inputs are finite; a program needn't handle non-finite values.
Results may differ from a plain program's by a relative error of at most 0.015.
Values may be sent and summed in bfloat16 or wider, within the bound.
A program may use at most 192 MiB of HBM per device.

v0:
```python
import jax
import jax.numpy as jnp
import numpy as np
from jax import lax
from jax.sharding import PartitionSpec as P

HEADS = 8
HEAD_DIM = 64
TILE = 8
HALO = 6


EPS_ROW = 1e-05
EPS_HEAD = 1e-06


def with_halo(value, sides, width, wrap):
    for axis, dim in sides:
        size, length = (lax.axis_size(axis), value.shape[dim])
        up = [(i, (i + 1) % size) for i in range(size if wrap else size - 1)]
        down = [(j, i) for i, j in up]
        last = lax.slice_in_dim(value, length - width, length, axis=dim)
        initial = lax.slice_in_dim(value, 0, width, axis=dim)
        before = lax.ppermute(last, axis, up)
        after = lax.ppermute(initial, axis, down)
        value = jnp.concatenate([before, value, after], axis=dim)
    return value


def head_norm(projected, head_gain):
    shaped = projected.reshape(projected.shape[:-1] + (HEADS, HEAD_DIM))
    inverse = lax.rsqrt(jnp.mean(shaped * shaped, axis=-1, keepdims=True) + EPS_HEAD)
    return (shaped * inverse * head_gain).reshape(projected.shape).astype(jnp.bfloat16)


def rms_rows(latents, norm_gain):
    widened = latents.astype(jnp.float32)
    inverse = lax.rsqrt(jnp.mean(widened * widened, axis=-1, keepdims=True) + EPS_ROW)
    return (widened * inverse * norm_gain).astype(jnp.bfloat16)


def band_mask(query_rows, query_cols):
    key_rows = query_rows + 2 * HALO
    key_cols = query_cols + 2 * HALO
    row_off = np.arange(key_rows)[None, :] - np.arange(query_rows)[:, None]
    col_off = np.arange(key_cols)[None, :] - np.arange(query_cols)[:, None]
    near_rows = (row_off >= 0) & (row_off <= 2 * HALO)
    near_cols = (col_off >= 0) & (col_off <= 2 * HALO)
    joined = near_rows[:, None, :, None] & near_cols[None, :, None, :]
    return joined.reshape(query_rows * query_cols, key_rows * key_cols)


def encode(fields, w_encode):
    cell_rows = fields.reshape(-1, fields.shape[-1])
    return jnp.dot(cell_rows, w_encode, preferred_element_type=jnp.float32).astype(jnp.bfloat16)


def extend(payload):
    beside_all = with_halo(payload, (("lon", 1),), HALO, True)
    return with_halo(beside_all, (("lat", 0),), HALO, False)


def per_device(
    fields, row_valid, w_encode, norm_gain, w_query, w_key, w_value, query_gain, key_gain, w_out
):
    lat_rows = fields.shape[0]
    lon_cols = fields.shape[1]
    att_width = w_query.shape[1]
    model_width = w_encode.shape[1]
    latents = encode(fields, w_encode)
    normed = rms_rows(latents, norm_gain)
    keys = head_norm(jnp.dot(normed, w_key, preferred_element_type=jnp.float32), key_gain)
    values = jnp.dot(normed, w_value, preferred_element_type=jnp.float32).astype(jnp.bfloat16)
    joined_kv = jnp.concatenate([keys, values], axis=-1).reshape(lat_rows, lon_cols, 2 * att_width)
    key_value = extend(joined_kv)
    queries = head_norm(jnp.dot(normed, w_query, preferred_element_type=jnp.float32), query_gain)
    queries = queries.reshape(lat_rows, lon_cols, att_width)
    lat_index = lax.axis_index("lat")
    rim_top = jnp.broadcast_to(lat_index > 0, (HALO,))
    bottom = jnp.broadcast_to(lat_index < lax.axis_size("lat") - 1, (HALO,))
    key_rows = jnp.concatenate([rim_top, row_valid == 1, bottom])
    tiles_lat = lat_rows // TILE
    group = tiles_lat
    for candidate in range(1, tiles_lat + 1):
        if tiles_lat % candidate == 0 and candidate * TILE * lon_cols >= 512:
            group = candidate
            break
    group_rows = group * TILE
    span_rows = group_rows + 2 * HALO
    span_cols = lon_cols + 2 * HALO
    static_mask = jnp.asarray(band_mask(group_rows, lon_cols))

    def attend(group_index):
        row_start = group_index * group_rows
        qblock = lax.dynamic_slice_in_dim(queries, row_start, group_rows, 0)
        qblock = qblock.reshape(group_rows * lon_cols, HEADS, HEAD_DIM)
        kblock = lax.dynamic_slice_in_dim(key_value, row_start, span_rows, 0)
        kblock = kblock.reshape(span_rows * span_cols, 2, HEADS, HEAD_DIM)
        rows_ok = lax.dynamic_slice_in_dim(key_rows, row_start, span_rows, 0)
        rows_ok = jnp.broadcast_to(rows_ok[:, None], (span_rows, span_cols)).reshape(1, -1)
        allowed = (static_mask & rows_ok)[None]
        scores = jnp.einsum(
            "qhd,khd->hqk", qblock, kblock[:, 0], preferred_element_type=jnp.float32
        ) * HEAD_DIM ** (-0.5)
        expo = jnp.where(allowed, jnp.exp(scores), 0.0)
        weights = (expo / jnp.sum(expo, axis=-1, keepdims=True)).astype(jnp.bfloat16)
        mixture = jnp.einsum(
            "hqk,khd->qhd", weights, kblock[:, 1], preferred_element_type=jnp.float32
        ).astype(jnp.bfloat16)
        return mixture.reshape(group_rows * lon_cols, att_width)

    mixture = lax.map(attend, jnp.arange(tiles_lat // group, dtype=jnp.int32)).reshape(
        -1, att_width
    )
    result = latents.astype(jnp.float32) + jnp.dot(
        mixture, w_out, preferred_element_type=jnp.float32
    )
    return result.astype(jnp.bfloat16).reshape(lat_rows, lon_cols, model_width)


def solution(mesh):
    return jax.shard_map(
        per_device,
        mesh=mesh,
        in_specs=(P("lat", "lon", None), P("lat"), P(), P(), P(), P(), P(), P(), P(), P()),
        out_specs=P("lat", "lon", None),
        check_vma=False,
    )
```

profile of v0, /device:TPU:1, one launch (start us, length us, event | category | flops | bytes accessed | tf_op | source)
XLA Modules:
  0.0 277.8 jit_solution(16165964274542491193)
XLA Ops:
  2.4 2.3 fusion.9
  4.8 2.7 convolution_convert_fusion.1
  7.5 2.9 %bitcast_reduce_fusion.1 = (f32[2048,8]{0,1:T(8,128)S(1)}, f32[2048,512]{0,1:T(8,128)S(1)}) fusion(bf16[1024,512]{1,0:T(8,128)(2,1)S(1)} %copy-done.8, bf16[2048,1024]{1,0:T(8,128)(2,1)S(1)} %get-tuple-element.91, f32[1024]{0:T(1024)S(1)} %copy-done.9, f32[2048]{0:T(1024)S(1)} %add_rsqrt_fusion.2), kind=kOutput, calls=%fused_computation.27 | convolution fusion | flops 2157953024 | bytes 9515008 | tf_op jit(solution)/shard_map/dot_general | solution.py:72
  10.9 2.5 pad_maximum_fusion.1
  13.4 6.5 %copy.26 = bf16[2048,1024]{1,0:T(8,128)(2,1)} copy(bf16[2048,1024]{0,1:T(8,128)(2,1)} %pad_maximum_fusion.1) | data formatting | bytes 8388608 | tf_op jit(solution)/shard_map/concatenate | solution.py:74
  19.9 3.0 %fusion.21 = (bf16[128,6,1024]{2,1,0:T(8,128)(2,1)S(1)}, bf16[128,6,1024]{2,1,0:T(8,128)(2,1)S(1)}) fusion(bf16[128,16,1024]{2,1,0:T(8,128)(2,1)} %bitcast.45), kind=kLoop, calls=%fused_computation.42 | loop fusion | bytes 6291456 | tf_op jit(solution)/shard_map/slice | solution.py:22
  23.8 11.4 %collective-permute-start.1 = (bf16[128,6,1024]{2,0,1:T(8,128)(2,1)S(1)}, bf16[128,6,1024]{2,0,1:T(8,128)(2,1)}, u32[]{:S(2)}, u32[]{:S(2)}) collective-permute-start(bf16[128,6,1024]{2,0,1:T(8,128)(2,1)S(1)} %copy.28), channel_id=1, source_target_pairs={{1,0},{2,1},{3,2},{4,3},{5,4},{6,5},{7,6},{8,7},{9,8},{10,9},{11,1... | collective-permute-start | bytes 4718600 | tf_op jit(solution)/shard_map/ppermute | solution.py:25
  37.3 7.8 %fusion.22 = (f32[2048,512]{1,0:T(8,128)}, f32[2048,512]{1,0:T(8,128)}) fusion(bf16[1024,512]{1,0:T(8,128)(2,1)S(1)} %copy-done, bf16[2048,1024]{1,0:T(8,128)(2,1)} %copy-done.11, f32[1024]{0:T(1024)S(1)} %copy-done.9, f32[2048]{0:T(1024)S(1)} %add_rsqrt_fusion.2), kind=kOutput, calls=%fused_computation.43 | convolution fusion | flops 2156920832 | bytes 13643776 | tf_op jit(solution)/shard_map/dot_general | solution.py:76
  45.1 5.4 %copy.31 = f32[2048,512]{0,1:T(8,128)} copy(f32[2048,512]{1,0:T(8,128)} %get-tuple-element.94) | data formatting | bytes 8388608 | tf_op jit(solution)/shard_map/mul | solution.py:32
  50.6 2.6 bitcast_reduce_fusion
  53.2 2.4 mul.104
  55.7 5.4 %copy.32 = f32[2048,512]{1,0:T(8,128)} copy(f32[2048,512]{0,1:T(8,128)} %bitcast.48) | data formatting | bytes 8388608 | tf_op jit(solution)/shard_map/mul | solution.py:33
  61.0 7.2 %collective-permute-done.1 = bf16[128,6,1024]{2,0,1:T(8,128)(2,1)} collective-permute-done((bf16[128,6,1024]{2,0,1:T(8,128)(2,1)S(1)}, bf16[128,6,1024]{2,0,1:T(8,128)(2,1)}, u32[]{:S(2)}, u32[]{:S(2)}) %collective-permute-start.1) | collective-permute-done | bytes 1572896 | tf_op jit(solution)/shard_map/ppermute | solution.py:25
  70.5 7.6 %collective-permute-done = bf16[128,6,1024]{2,0,1:T(8,128)(2,1)} collective-permute-done((bf16[128,6,1024]{2,0,1:T(8,128)(2,1)}, bf16[128,6,1024]{2,0,1:T(8,128)(2,1)}, u32[]{:S(2)}, u32[]{:S(2)}) %collective-permute-start) | collective-permute-done | bytes 1572896 | tf_op jit(solution)/shard_map/ppermute | solution.py:24
  81.8 4.2 %collective-permute-start.2 = (bf16[6,28,1024]{2,1,0:T(8,128)(2,1)S(1)}, bf16[6,28,1024]{2,1,0:T(8,128)(2,1)S(1)}, u32[]{:S(2)}, u32[]{:S(2)}) collective-permute-start(bf16[6,28,1024]{2,1,0:T(8,128)(2,1)S(1)} %get-tuple-element.86), channel_id=1, source_target_pairs={{0,64},{64,128},{128,192},{1,65},{65,129},{129,193},{2,66},{66,130... | collective-permute-start | bytes 1032200 | tf_op jit(solution)/shard_map/ppermute | solution.py:24
  88.0 2.5 multiply_convert_fusion
  90.7 4.5 %collective-permute-done.3 = bf16[6,28,1024]{2,1,0:T(8,128)(2,1)} collective-permute-done((bf16[6,28,1024]{2,1,0:T(8,128)(2,1)S(1)}, bf16[6,28,1024]{2,1,0:T(8,128)(2,1)}, u32[]{:S(2)}, u32[]{:S(2)}) %collective-permute-start.3) | collective-permute-done | bytes 344096 | tf_op jit(solution)/shard_map/ppermute | solution.py:25
  95.2 12.5 %pad_maximum_fusion = bf16[140,28,1024]{2,1,0:T(8,128)(2,1)} fusion(bf16[6,28,1024]{2,1,0:T(8,128)(2,1)} %collective-permute-done.3, bf16[128,6,1024]{2,1,0:T(8,128)(2,1)S(1)} %copy.30, bf16[128,16,1024]{2,1,0:T(8,128)(2,1)} %bitcast.46, bf16[128,6,1024]{2,1,0:T(8,128)(2,1)} %copy-done.3, bf16[6,28,1024]{2,1,0:T(8,128)(2,1)S(1)} %collective-permute-done.2), kind=kLoop, calls=%fused_computation.17 | loop fusion | flops 40140800 | bytes 16056320 | tf_op jit(solution)/shard_map/concatenate | solution.py:26
  107.7 162.4 %while.11 = (s32[]{:T(128)}, bf16[4,512,512]{2,1,0:T(8,128)(2,1)}, s32[4]{0:T(128)S(1)}, bf16[140,28,1024]{2,1,0:T(8,128)(2,1)}, pred[140]{0:T(512)(128)(4,1)S(1...) while((s32[]{:T(128)}, bf16[4,512,512]{2,1,0:T(8,128)(2,1)}, ...), condition=%wide.region_5.6_spmd.clone, body=%wide.region_3.5_spmd.sunk.clone.sunk | while | flops 1323012096 | bytes 70882472 | solution.py:112
  112.4 3.9 %constant_dynamic-slice_fusion.4 = bf16[44,28,1024]{2,1,0:T(8,128)(2,1)} fusion(bf16[140,28,1024]{2,1,0:T(8,128)(2,1)} %get-tuple-element.168, s32[]{:T(128)S(6)} %select_n.31), kind=kLoop, calls=%fused_computation.12.clone.1 | loop fusion | bytes 5046276 | tf_op jit(solution)/shard_map/while/body/eval_jaxpr/dynamic_slice | solution.py:97
  116.3 7.7 %reshape.97 = bf16[1232,2,8,64]{3,2,1,0:T(8,128)(2,1)} reshape(bf16[44,28,1024]{2,1,0:T(8,128)(2,1)} %constant_dynamic-slice_fusion.4) | data formatting | bytes 5046272 | tf_op jit(solution)/shard_map/while/body/eval_jaxpr/reshape | solution.py:98
  124.0 4.1 %fusion.35 = (bf16[1232,1,8,64]{3,2,1,0:T(8,128)(2,1)}, bf16[1232,1,8,64]{3,2,1,0:T(8,128)(2,1)}) fusion(bf16[1232,2,8,64]{3,2,1,0:T(8,128)(2,1)} %reshape.97), kind=kLoop, calls=%fused_computation.41.clone.1 | loop fusion | bytes 5046272 | tf_op jit(solution)/shard_map/while/body/eval_jaxpr/slice | solution.py:108
  128.1 4.5 %copy.47 = bf16[1232,1,8,64]{0,3,2,1:T(8,128)(2,1)} copy(bf16[1232,1,8,64]{3,2,1,0:T(8,128)(2,1)} %get-tuple-element.137) | data formatting | bytes 2523136 | tf_op jit(solution)/shard_map/while
  132.6 3.6 %copy.48 = bf16[1232,1,8,64]{0,3,2,1:T(8,128)(2,1)S(1)} copy(bf16[1232,1,8,64]{3,2,1,0:T(8,128)(2,1)} %get-tuple-element.140) | data formatting | bytes 2523136 | tf_op jit(solution)/shard_map/while
  136.2 6.7 %fusion.36 = (f32[8,512]{1,0:T(8,128)S(1)}, f32[8,512,1232]{1,2,0:T(8,128)S(1)}) fusion(pred[512,1232]{0,1:T(8,128)(4,1)S(1)} %broadcast_and_fusion.2, bf16[1232,1,8,64]{0,3,2,1:T(8,128)(2,1)} %copy.47, bf16[512,8,64]{2,1,0:T(8,128)(2,1)S(1)} %reshape.98), kind=kOutput, calls=%fused_computation.3.clone.1 | convolution fusion | flops 661057536 | bytes 22618112 | tf_op jit(solution)/shard_map/while/body/eval_jaxpr/qhd,khd->hqk/dot_general | solution.py:102
  142.9 4.4 %fusion.37 = bf16[8,64,512]{2,1,0:T(8,128)(2,1)S(1)} fusion(f32[8,512,1232]{1,2,0:T(8,128)S(1)} %get-tuple-element.138, f32[8,512]{1,0:T(8,128)S(1)} %get-tuple-element.139, pred[512,1232]{0,1:T(8,128)(4,1)S(1)} %broadcast_and_fusion.2, bf16[1232,1,8,64]{0,3,2,1:T(8,128)(2,1)S(1)} %copy.48), kind=kOutput, calls=%fused_computation.7.clone.1 | convolution fusion | flops 661323776 | bytes 22618112 | tf_op jit(solution)/shard_map/while/body/eval_jaxpr/hqk,khd->qhd/dot_general | solution.py:107
  153.1 3.9 %constant_dynamic-slice_fusion.4 = bf16[44,28,1024]{2,1,0:T(8,128)(2,1)} fusion(bf16[140,28,1024]{2,1,0:T(8,128)(2,1)} %get-tuple-element.168, s32[]{:T(128)S(6)} %select_n.31), kind=kLoop, calls=%fused_computation.12.clone.1 | loop fusion | bytes 5046276 | tf_op jit(solution)/shard_map/while/body/eval_jaxpr/dynamic_slice | solution.py:97
  156.9 7.7 %reshape.97 = bf16[1232,2,8,64]{3,2,1,0:T(8,128)(2,1)} reshape(bf16[44,28,1024]{2,1,0:T(8,128)(2,1)} %constant_dynamic-slice_fusion.4) | data formatting | bytes 5046272 | tf_op jit(solution)/shard_map/while/body/eval_jaxpr/reshape | solution.py:98
  164.6 4.1 %fusion.35 = (bf16[1232,1,8,64]{3,2,1,0:T(8,128)(2,1)}, bf16[1232,1,8,64]{3,2,1,0:T(8,128)(2,1)}) fusion(bf16[1232,2,8,64]{3,2,1,0:T(8,128)(2,1)} %reshape.97), kind=kLoop, calls=%fused_computation.41.clone.1 | loop fusion | bytes 5046272 | tf_op jit(solution)/shard_map/while/body/eval_jaxpr/slice | solution.py:108
  168.7 4.5 %copy.47 = bf16[1232,1,8,64]{0,3,2,1:T(8,128)(2,1)} copy(bf16[1232,1,8,64]{3,2,1,0:T(8,128)(2,1)} %get-tuple-element.137) | data formatting | bytes 2523136 | tf_op jit(solution)/shard_map/while
  173.2 3.6 %copy.48 = bf16[1232,1,8,64]{0,3,2,1:T(8,128)(2,1)S(1)} copy(bf16[1232,1,8,64]{3,2,1,0:T(8,128)(2,1)} %get-tuple-element.140) | data formatting | bytes 2523136 | tf_op jit(solution)/shard_map/while
  176.8 6.7 %fusion.36 = (f32[8,512]{1,0:T(8,128)S(1)}, f32[8,512,1232]{1,2,0:T(8,128)S(1)}) fusion(pred[512,1232]{0,1:T(8,128)(4,1)S(1)} %broadcast_and_fusion.2, bf16[1232,1,8,64]{0,3,2,1:T(8,128)(2,1)} %copy.47, bf16[512,8,64]{2,1,0:T(8,128)(2,1)S(1)} %reshape.98), kind=kOutput, calls=%fused_computation.3.clone.1 | convolution fusion | flops 661057536 | bytes 22618112 | tf_op jit(solution)/shard_map/while/body/eval_jaxpr/qhd,khd->hqk/dot_general | solution.py:102
  183.5 4.4 %fusion.37 = bf16[8,64,512]{2,1,0:T(8,128)(2,1)S(1)} fusion(f32[8,512,1232]{1,2,0:T(8,128)S(1)} %get-tuple-element.138, f32[8,512]{1,0:T(8,128)S(1)} %get-tuple-element.139, pred[512,1232]{0,1:T(8,128)(4,1)S(1)} %broadcast_and_fusion.2, bf16[1232,1,8,64]{0,3,2,1:T(8,128)(2,1)S(1)} %copy.48), kind=kOutput, calls=%fused_computation.7.clone.1 | convolution fusion | flops 661323776 | bytes 22618112 | tf_op jit(solution)/shard_map/while/body/eval_jaxpr/hqk,khd->qhd/dot_general | solution.py:107
  193.7 3.9 %constant_dynamic-slice_fusion.4 = bf16[44,28,1024]{2,1,0:T(8,128)(2,1)} fusion(bf16[140,28,1024]{2,1,0:T(8,128)(2,1)} %get-tuple-element.168, s32[]{:T(128)S(6)} %select_n.31), kind=kLoop, calls=%fused_computation.12.clone.1 | loop fusion | bytes 5046276 | tf_op jit(solution)/shard_map/while/body/eval_jaxpr/dynamic_slice | solution.py:97
  197.5 7.7 %reshape.97 = bf16[1232,2,8,64]{3,2,1,0:T(8,128)(2,1)} reshape(bf16[44,28,1024]{2,1,0:T(8,128)(2,1)} %constant_dynamic-slice_fusion.4) | data formatting | bytes 5046272 | tf_op jit(solution)/shard_map/while/body/eval_jaxpr/reshape | solution.py:98
  205.3 4.1 %fusion.35 = (bf16[1232,1,8,64]{3,2,1,0:T(8,128)(2,1)}, bf16[1232,1,8,64]{3,2,1,0:T(8,128)(2,1)}) fusion(bf16[1232,2,8,64]{3,2,1,0:T(8,128)(2,1)} %reshape.97), kind=kLoop, calls=%fused_computation.41.clone.1 | loop fusion | bytes 5046272 | tf_op jit(solution)/shard_map/while/body/eval_jaxpr/slice | solution.py:108
  209.4 4.5 %copy.47 = bf16[1232,1,8,64]{0,3,2,1:T(8,128)(2,1)} copy(bf16[1232,1,8,64]{3,2,1,0:T(8,128)(2,1)} %get-tuple-element.137) | data formatting | bytes 2523136 | tf_op jit(solution)/shard_map/while
  213.8 3.6 %copy.48 = bf16[1232,1,8,64]{0,3,2,1:T(8,128)(2,1)S(1)} copy(bf16[1232,1,8,64]{3,2,1,0:T(8,128)(2,1)} %get-tuple-element.140) | data formatting | bytes 2523136 | tf_op jit(solution)/shard_map/while
  217.4 6.7 %fusion.36 = (f32[8,512]{1,0:T(8,128)S(1)}, f32[8,512,1232]{1,2,0:T(8,128)S(1)}) fusion(pred[512,1232]{0,1:T(8,128)(4,1)S(1)} %broadcast_and_fusion.2, bf16[1232,1,8,64]{0,3,2,1:T(8,128)(2,1)} %copy.47, bf16[512,8,64]{2,1,0:T(8,128)(2,1)S(1)} %reshape.98), kind=kOutput, calls=%fused_computation.3.clone.1 | convolution fusion | flops 661057536 | bytes 22618112 | tf_op jit(solution)/shard_map/while/body/eval_jaxpr/qhd,khd->hqk/dot_general | solution.py:102
  224.1 4.4 %fusion.37 = bf16[8,64,512]{2,1,0:T(8,128)(2,1)S(1)} fusion(f32[8,512,1232]{1,2,0:T(8,128)S(1)} %get-tuple-element.138, f32[8,512]{1,0:T(8,128)S(1)} %get-tuple-element.139, pred[512,1232]{0,1:T(8,128)(4,1)S(1)} %broadcast_and_fusion.2, bf16[1232,1,8,64]{0,3,2,1:T(8,128)(2,1)S(1)} %copy.48), kind=kOutput, calls=%fused_computation.7.clone.1 | convolution fusion | flops 661323776 | bytes 22618112 | tf_op jit(solution)/shard_map/while/body/eval_jaxpr/hqk,khd->qhd/dot_general | solution.py:107
  234.3 3.9 %constant_dynamic-slice_fusion.4 = bf16[44,28,1024]{2,1,0:T(8,128)(2,1)} fusion(bf16[140,28,1024]{2,1,0:T(8,128)(2,1)} %get-tuple-element.168, s32[]{:T(128)S(6)} %select_n.31), kind=kLoop, calls=%fused_computation.12.clone.1 | loop fusion | bytes 5046276 | tf_op jit(solution)/shard_map/while/body/eval_jaxpr/dynamic_slice | solution.py:97
  238.1 7.7 %reshape.97 = bf16[1232,2,8,64]{3,2,1,0:T(8,128)(2,1)} reshape(bf16[44,28,1024]{2,1,0:T(8,128)(2,1)} %constant_dynamic-slice_fusion.4) | data formatting | bytes 5046272 | tf_op jit(solution)/shard_map/while/body/eval_jaxpr/reshape | solution.py:98
  245.9 4.1 %fusion.35 = (bf16[1232,1,8,64]{3,2,1,0:T(8,128)(2,1)}, bf16[1232,1,8,64]{3,2,1,0:T(8,128)(2,1)}) fusion(bf16[1232,2,8,64]{3,2,1,0:T(8,128)(2,1)} %reshape.97), kind=kLoop, calls=%fused_computation.41.clone.1 | loop fusion | bytes 5046272 | tf_op jit(solution)/shard_map/while/body/eval_jaxpr/slice | solution.py:108
  250.0 4.5 %copy.47 = bf16[1232,1,8,64]{0,3,2,1:T(8,128)(2,1)} copy(bf16[1232,1,8,64]{3,2,1,0:T(8,128)(2,1)} %get-tuple-element.137) | data formatting | bytes 2523136 | tf_op jit(solution)/shard_map/while
  254.4 3.6 %copy.48 = bf16[1232,1,8,64]{0,3,2,1:T(8,128)(2,1)S(1)} copy(bf16[1232,1,8,64]{3,2,1,0:T(8,128)(2,1)} %get-tuple-element.140) | data formatting | bytes 2523136 | tf_op jit(solution)/shard_map/while
  258.0 6.7 %fusion.36 = (f32[8,512]{1,0:T(8,128)S(1)}, f32[8,512,1232]{1,2,0:T(8,128)S(1)}) fusion(pred[512,1232]{0,1:T(8,128)(4,1)S(1)} %broadcast_and_fusion.2, bf16[1232,1,8,64]{0,3,2,1:T(8,128)(2,1)} %copy.47, bf16[512,8,64]{2,1,0:T(8,128)(2,1)S(1)} %reshape.98), kind=kOutput, calls=%fused_computation.3.clone.1 | convolution fusion | flops 661057536 | bytes 22618112 | tf_op jit(solution)/shard_map/while/body/eval_jaxpr/qhd,khd->hqk/dot_general | solution.py:102
  264.7 4.4 %fusion.37 = bf16[8,64,512]{2,1,0:T(8,128)(2,1)S(1)} fusion(f32[8,512,1232]{1,2,0:T(8,128)S(1)} %get-tuple-element.138, f32[8,512]{1,0:T(8,128)S(1)} %get-tuple-element.139, pred[512,1232]{0,1:T(8,128)(4,1)S(1)} %broadcast_and_fusion.2, bf16[1232,1,8,64]{0,3,2,1:T(8,128)(2,1)S(1)} %copy.48), kind=kOutput, calls=%fused_computation.7.clone.1 | convolution fusion | flops 661323776 | bytes 22618112 | tf_op jit(solution)/shard_map/while/body/eval_jaxpr/hqk,khd->qhd/dot_general | solution.py:107
  270.2 7.6 %fusion.12 = bf16[2048,1024]{1,0:T(8,128)(2,1)} fusion(bf16[2048,1024]{1,0:T(8,128)(2,1)} %copy-done.11, bf16[2048,512]{1,0:T(8,128)(2,1)} %bitcast.52, bf16[512,1024]{1,0:T(8,128)(2,1)} %param.22), kind=kOutput, calls=%fused_computation.21 | convolution fusion | flops 2153775104 | bytes 11534336 | tf_op jit(solution)/shard_map/dot_general | solution.py:115
  (83 shorter events, 34.1 us)
Async XLA Ops:
  0.0 37.3 %copy-start = (bf16[1024,512]{1,0:T(8,128)(2,1)S(1)}, bf16[1024,512]{1,0:T(8,128)(2,1)}, u32[]{:S(2)}) copy-start(bf16[1024,512]{1,0:T(8,128)(2,1)} %param.17) | copy-start | bytes 3145732
  0.0 4.7 %copy-start.9 = (f32[1024]{0:T(1024)S(1)}, f32[1024]{0:T(1024)}, u32[]{:S(2)}) copy-start(f32[1024]{0:T(1024)} %param.16) | copy-start | bytes 12292
  2.4 2.4 copy-start.7
  4.7 2.8 %copy-start.11 = (bf16[2048,1024]{1,0:T(8,128)(2,1)}, bf16[2048,1024]{1,0:T(8,128)(2,1)S(1)}, u32[]{:S(2)}) copy-start(bf16[2048,1024]{1,0:T(8,128)(2,1)S(1)} %get-tuple-element.91) | copy-start | bytes 12582916
  4.7 2.8 copy-start.8
  22.9 14.3 %copy-start.6 = (f32[64]{0:T(128)S(1)}, f32[64]{0:T(128)}, u32[]{:S(2)}) copy-start(f32[64]{0:T(128)} %param.20) | copy-start | bytes 772
  23.8 44.5 %collective-permute-start.1 = (bf16[128,6,1024]{2,0,1:T(8,128)(2,1)S(1)}, bf16[128,6,1024]{2,0,1:T(8,128)(2,1)}, u32[]{:S(2)}, u32[]{:S(2)}) collective-permute-start(bf16[128,6,1024]{2,0,1:T(8,128)(2,1)S(1)} %copy.28), channel_id=1, source_target_pairs={{1,0},{2,1},{3,2},{4,3},{5,4},{6,5},{7,6},{8,7},{9,8},{10,9},{11,1... | collective-permute-start | bytes 4718600 | tf_op jit(solution)/shard_map/ppermute | solution.py:25
  37.2 41.0 %collective-permute-start = (bf16[128,6,1024]{2,0,1:T(8,128)(2,1)}, bf16[128,6,1024]{2,0,1:T(8,128)(2,1)}, u32[]{:S(2)}, u32[]{:S(2)}) collective-permute-start(bf16[128,6,1024]{2,0,1:T(8,128)(2,1)} %copy.27), channel_id=1, source_target_pairs={{0,1},{1,2},{2,3},{3,4},{4,5},{5,6},{6,7},{7,8},{8,9},{9,10},{10,1... | collective-permute-start | bytes 4718600 | tf_op jit(solution)/shard_map/ppermute | solution.py:24
  61.0 19.4 %copy-start.2 = (bf16[2048,1024]{1,0:T(8,128)(2,1)S(1)}, bf16[2048,1024]{1,0:T(8,128)(2,1)}, u32[]{:S(2)}) copy-start(bf16[2048,1024]{1,0:T(8,128)(2,1)} %copy.26) | copy-start | bytes 12582916
  80.5 1.3 copy-start.3
  80.5 7.5 %copy-start.4 = (f32[2048,512]{1,0:T(8,128)S(1)}, f32[2048,512]{1,0:T(8,128)}, u32[]{:S(2)}) copy-start(f32[2048,512]{1,0:T(8,128)} %copy.32) | copy-start | bytes 12582916
  80.5 7.5 %copy-start.5 = (f32[2048,512]{1,0:T(8,128)S(1)}, f32[2048,512]{1,0:T(8,128)}, u32[]{:S(2)}) copy-start(f32[2048,512]{1,0:T(8,128)} %get-tuple-element.95) | copy-start | bytes 12582916
  81.8 8.9 %collective-permute-start.2 = (bf16[6,28,1024]{2,1,0:T(8,128)(2,1)S(1)}, bf16[6,28,1024]{2,1,0:T(8,128)(2,1)S(1)}, u32[]{:S(2)}, u32[]{:S(2)}) collective-permute-start(bf16[6,28,1024]{2,1,0:T(8,128)(2,1)S(1)} %get-tuple-element.86), channel_id=1, source_target_pairs={{0,64},{64,128},{128,192},{1,65},{65,129},{129,193},{2,66},{66,130... | collective-permute-start | bytes 1032200 | tf_op jit(solution)/shard_map/ppermute | solution.py:24
  86.0 9.2 %collective-permute-start.3 = (bf16[6,28,1024]{2,1,0:T(8,128)(2,1)S(1)}, bf16[6,28,1024]{2,1,0:T(8,128)(2,1)}, u32[]{:S(2)}, u32[]{:S(2)}) collective-permute-start(bf16[6,28,1024]{2,1,0:T(8,128)(2,1)S(1)} %get-tuple-element.87), channel_id=1, source_target_pairs={{64,0},{128,64},{192,128},{65,1},{129,65},{193,129},{66,2},{130,66... | collective-permute-start | bytes 1032200 | tf_op jit(solution)/shard_map/ppermute | solution.py:25
  88.0 2.5 copy-start.10
  270.2 7.6 %copy-start.1 = (bf16[1024,512]{1,0:T(8,128)(2,1)S(1)}, bf16[1024,512]{1,0:T(8,128)(2,1)}, u32[]{:S(2)}) copy-start(bf16[1024,512]{1,0:T(8,128)(2,1)} %param.17) | copy-start | bytes 3145732
where the time goes:
time: 280 us; the launch traced here: 278 us
  local copies, waits for them, and re-layouts  143 us (51%)
  matrix products  67.5 us (24%)
  other arithmetic  27 us (10%)
  waiting for transfers between devices  19.5 us (7%)
  starting transfers between devices  17.5 us (6%)
  loops' own time  2.94 us (1%)
    while x8, local copies, waits for them, and re-layouts  32.3 us
    reshape x4, local copies, waits for them, and re-layouts, attend(): kblock = kblock.reshape(span_rows * span_cols, 2, HEADS, HEAD_DIM)  31 us
    dot_general x4, matrix products, attend(): jnp.einsum('qhd,khd->hqk', qblock, kblock[:, 0], preferred_element_type=j...  26.7 us
    dot_general x4, matrix products, attend(): jnp.einsum('hqk,khd->qhd', weights, kblock[:, 1], preferred_element_type=...  17.5 us
    slice x4, local copies, waits for them, and re-layouts, attend(): kblock[:, 1]  16.4 us
    dynamic_slice x4, local copies, waits for them, and re-layouts, attend(): kblock = lax.dynamic_slice_in_dim(key_value, row_start, span_rows, 0)  15.4 us
    ppermute x2, starting transfers between devices, with_halo(): after = lax.ppermute(initial, axis, down)  13.3 us
    concatenate x1, other arithmetic, with_halo(): value = jnp.concatenate([before, value, after], axis=dim)  12.5 us
  transfers between devices with their start and end apart: 4, of which 4 were waited for; matrix products, arithmetic and copies ran while one was open for 11% of the time, Pallas kernels for 0%

commit v1 on v0

v1 whole, which is shorter than its diff:
```python
import functools
import math

import jax
import jax.numpy as jnp
from jax import lax
from jax.experimental import pallas as pl
from jax.experimental.pallas import tpu as pltpu
from jax.sharding import PartitionSpec as P

HEADS = 8
HEAD_DIM = 64
HALO = 6
TR = 4
SIDE = 8
EPS_ROW = 1e-05
EPS_HEAD = 1e-06
F32 = jnp.float32
BF16 = jnp.bfloat16
MESH = pl.DeviceIdType.MESH
NT = (((1,), (1,)), ((), ()))


def nn(a, b):
    return jnp.dot(a, b, preferred_element_type=F32)


def nt(a, b):
    return lax.dot_general(a, b, NT, preferred_element_type=F32)


def split(x):
    hi = x.astype(BF16)
    return hi, (x - hi.astype(F32)).astype(BF16)


def chunk_of(count, most):
    return max(c for c in range(1, most + 1) if count % c == 0)


def attend_kernel(
    n_lat, n_lon, rows, cols, chan, hd,
    fields, valid, w_enc, gain, w_q, w_k, w_v, q_gain, k_gain,
    mix,
    fraw, fext, send_l, send_r, halo_l, halo_r, enc, wq, wk, wv, comp, ones_blk,
    q_s, k_o, v_o, k_l, v_l, k_r, v_r, masks,
    local_sem, send_sem, recv_sem,
):
    lat, lon = lax.axis_index("lat"), lax.axis_index("lon")
    up, down = lax.rem(lat + n_lat - 1, n_lat), lax.rem(lat + 1, n_lat)
    left, right = lax.rem(lon + n_lon - 1, n_lon), lax.rem(lon + 1, n_lon)
    pairs = rows // 2
    ext = rows + 2 * HALO
    tiles = rows // TR
    hp = HALO // 2

    loads = [
        pltpu.make_async_copy(src, dst, local_sem.at[i])
        for i, (src, dst) in enumerate(
            ((fields, fraw), (w_enc, enc), (w_k, wk), (w_v, wv), (w_q, wq))
        )
    ]
    for load in loads:
        load.start()

    barrier = pltpu.get_barrier_semaphore()
    around = [
        (up, left), (up, lon), (up, right), (lat, left), (lat, right), (down, left), (down, lon), (down, right)
    ]
    for dev in around:
        pl.semaphore_signal(barrier, inc=1, device_id=dev, device_id_type=MESH)

    own = pl.ds(HALO, rows)
    fext[own] = jnp.zeros((rows, cols, 128), BF16)
    send_l[...] = jnp.zeros(send_l.shape, BF16)
    send_r[...] = jnp.zeros(send_r.shape, BF16)
    loads[0].wait()

    def pack(i, c):
        x = fraw[pl.ds(i * 8, 8)]
        fext[pl.ds(HALO + i * 8, 8), :, 0:chan] = x
        x = x.astype(F32)
        send_l[pl.ds(i * 4, 4), :, 0:chan] = x[:, 0:SIDE].reshape(4, 16, chan).astype(BF16)
        send_r[pl.ds(i * 4, 4), :, 0:chan] = x[:, cols - SIDE :].reshape(4, 16, chan).astype(BF16)
        return c

    lax.fori_loop(0, rows // 8, pack, 0)
    pl.semaphore_wait(barrier, 8)

    first, last = pl.ds(0, hp), pl.ds(pairs - hp, hp)
    top, mid, bot = pl.ds(0, hp), pl.ds(hp, pairs), pl.ds(hp + pairs, hp)
    plan = [
        (send_l.at[...], halo_r.at[mid], (lat, left)),
        (send_r.at[...], halo_l.at[mid], (lat, right)),
        (fext.at[pl.ds(HALO, HALO)], fext.at[pl.ds(HALO + rows, HALO)], (up, lon)),
        (fext.at[pl.ds(rows, HALO)], fext.at[pl.ds(0, HALO)], (down, lon)),
        (send_l.at[first], halo_r.at[bot], (up, left)),
        (send_l.at[last], halo_r.at[top], (down, left)),
        (send_r.at[first], halo_l.at[bot], (up, right)),
        (send_r.at[last], halo_l.at[top], (down, right)),
    ]
    copies = [
        pltpu.make_async_remote_copy(
            src_ref=src, dst_ref=dst, send_sem=send_sem.at[i], recv_sem=recv_sem.at[i],
            device_id=dev, device_id_type=MESH,
        )
        for i, (src, dst, dev) in enumerate(plan)
    ]
    for copy in copies:
        copy.start()

    comp[...] = jnp.zeros(comp.shape, BF16)
    row_i = lax.broadcasted_iota(jnp.int32, (256, 256), 0) // HEAD_DIM
    col_i = lax.broadcasted_iota(jnp.int32, (256, 256), 1) // HEAD_DIM
    ones_blk[...] = jnp.where(row_i == col_i, 1.0 / HEAD_DIM, 0.0).astype(BF16)

    keys = (TR + 2 * HALO) * (cols + 2 * SIDE)
    half = (TR + 2 * HALO) * cols
    side = (TR + 2 * HALO) * SIDE
    lane = lax.broadcasted_iota(jnp.int32, (1, keys), 1)
    rel = jnp.where(lane < half, lane, jnp.where(lane < half + side, lane - half, lane - half - side))
    key_row = jnp.where(lane < half, rel // cols, rel // SIDE)
    key_col = jnp.where(
        lane < half, rel % cols, jnp.where(lane < half + side, rel % SIDE - SIDE, rel % SIDE + cols)
    )
    qi = lax.broadcasted_iota(jnp.int32, (TR * cols, 1), 0)
    row_off = key_row - qi // cols
    col_off = key_col - qi % cols
    near = (row_off >= 0) & (row_off <= 2 * HALO) & (col_off >= -HALO) & (col_off <= HALO)
    base = jnp.where(near, 1.0, 0.0).astype(F32)
    has_up = jnp.where(lat > 0, 1.0, 0.0).astype(F32)
    has_down = jnp.where(lat < n_lat - 1, 1.0, 0.0).astype(F32)
    for slot, tile in enumerate((0, 1, 2, None, tiles - 3, tiles - 2, tiles - 1)):
        m = base
        if tile is not None:
            ok = jnp.ones((1, keys), F32)
            for r in range(TR + 2 * HALO):
                e = tile * TR + r
                if e < HALO:
                    v = has_up
                elif e >= HALO + rows:
                    v = has_down
                else:
                    v = valid[e - HALO].astype(F32)
                ok = jnp.where(key_row == r, v, ok)
            m = base * ok
        masks[slot] = m.astype(BF16)

    loads[1].wait()
    enc_v = enc[...]
    wg_hi, wg_lo = split(enc_v.astype(F32) * gain[...])

    def put(x, at):
        hi, lo = split(x)
        comp[0 : x.shape[0], at : at + x.shape[1]] = hi
        comp[128 : 128 + x.shape[0], at : at + x.shape[1]] = lo

    put(nt(enc_v, enc_v) * (1.0 / enc_v.shape[1]), 2 * hd)
    for load, w, at in ((loads[2], wk, 0), (loads[3], wv, hd), (loads[4], wq, 2 * hd + 128)):
        load.wait()
        put(nn(wg_hi, w[...]) + nn(wg_lo, w[...]), at)

    def tiled(g):
        pair = jnp.concatenate([g[...]] * 2, axis=1)
        return jnp.concatenate([pair] * (hd // 128), axis=1)

    kg = tiled(k_gain)
    qg = tiled(q_gain) * (math.log2(math.e) / math.sqrt(HEAD_DIM))

    def head_norm(x, eps_u, g):
        sq = (x * x).astype(BF16)
        blk = ones_blk[...]
        mean = jnp.concatenate([nn(sq[:, i : i + 256], blk) for i in range(0, hd, 256)], axis=1)
        return (x * lax.rsqrt(mean + eps_u) * g).astype(BF16)

    def project(f, k_ref, v_ref, at, q_at=None):
        n = f.shape[0]
        two = jnp.concatenate([f, f], axis=1)
        width = 2 * hd + 128 + (hd if q_at is not None else 0)
        y = nn(two, comp[:, 0:width])
        quad = jnp.sum(y[:, 2 * hd : 2 * hd + 128] * f.astype(F32), axis=1, keepdims=True)
        u = jnp.maximum(quad, 0.0) + EPS_ROW
        eps_u = EPS_HEAD * u
        k_ref[pl.ds(at, n), :] = head_norm(y[:, 0:hd], eps_u, kg)
        v_ref[pl.ds(at, n), :] = (y[:, hd : 2 * hd] * lax.rsqrt(u)).astype(BF16)
        if q_at is not None:
            q_s[pl.ds(q_at, n), :] = head_norm(y[:, 2 * hd + 128 :], eps_u, qg)

    crow = chunk_of(rows, 16)
    ccell = crow * cols

    def own_step(i, c):
        f = fext[pl.ds(HALO + i * crow, crow)].reshape(ccell, 128)
        project(f, k_o, v_o, pl.multiple_of(HALO * cols + i * ccell, 16), pl.multiple_of(i * ccell, 16))
        return c

    lax.fori_loop(0, rows // crow, own_step, 0)

    for copy in copies:
        copy.wait_recv()

    for r0 in (0, HALO + rows):
        project(fext[r0 : r0 + HALO].reshape(HALO * cols, 128), k_o, v_o, r0 * cols)

    cpair = chunk_of(pairs + 2 * hp, 14)

    def side_step(i, c):
        for src, k_ref, v_ref in ((halo_l, k_l, v_l), (halo_r, k_r, v_r)):
            f = src[pl.ds(i * cpair, cpair)].reshape(cpair * 16, 128)
            project(f, k_ref, v_ref, pl.multiple_of(i * cpair * 16, 16))
        return c

    lax.fori_loop(0, (pairs + 2 * hp) // cpair, side_step, 0)

    nq = TR * cols
    head = lax.broadcasted_iota(jnp.int32, (nq, 256), 1) // HEAD_DIM

    def attend(t, c):
        slot = jnp.minimum(t, 3) + jnp.maximum(t - (tiles - 4), 0)
        m = masks[slot]
        m4 = jnp.concatenate([m] * 4, axis=0)
        o_at = pl.ds(pl.multiple_of(t * nq, nq), half)
        s_at = pl.ds(pl.multiple_of(t * TR * SIDE, TR * SIDE), side)
        q_at = pl.ds(pl.multiple_of(t * nq, nq), nq)
        for p in range(hd // 256):
            ps = slice(256 * p, 256 * p + 256)
            q = q_s[q_at, ps]
            zero = jnp.zeros_like(q)
            q4 = jnp.concatenate([jnp.where(head == h, q, zero) for h in range(4)], axis=0)
            k = jnp.concatenate([k_o[o_at, ps], k_l[s_at, ps], k_r[s_at, ps]], axis=0)
            v = jnp.concatenate([v_o[o_at, ps], v_l[s_at, ps], v_r[s_at, ps]], axis=0)
            e = jnp.exp2(nt(q4, k)).astype(BF16) * m4
            den = jnp.sum(e.astype(F32), axis=1, keepdims=True)
            acc = nn(e, v) * (1.0 / den)
            out = acc[0:nq]
            for h in range(1, 4):
                out = jnp.where(head == h, acc[h * nq : (h + 1) * nq], out)
            mix[q_at, ps] = out.astype(BF16)
        return c

    lax.fori_loop(0, tiles, attend, 0, unroll=2)

    for copy in copies:
        copy.wait_send()


def out_kernel(fields, w_enc, mix, w_out, out):
    f = fields[...]
    n = f.shape[0] * f.shape[1]
    latents = nn(f.reshape(n, f.shape[2]), w_enc[...]).astype(BF16)
    res = latents.astype(F32) + nn(mix[...], w_out[...])
    out[...] = res.astype(BF16).reshape(out.shape)


def per_device(n_lat, n_lon, fields, row_valid, w_encode, norm_gain, w_query, w_key, w_value, query_gain, key_gain, w_out):
    rows, cols, chan = fields.shape
    d, hd = w_query.shape
    cells = rows * cols
    ext = rows + 2 * HALO
    pairs = ext // 2
    any_spec = pl.BlockSpec(memory_space=pl.ANY)
    vmem = pl.BlockSpec(memory_space=pltpu.VMEM)
    keys = (TR + 2 * HALO) * (cols + 2 * SIDE)
    mix = pl.pallas_call(
        functools.partial(attend_kernel, n_lat, n_lon, rows, cols, chan, hd),
        out_shape=jax.ShapeDtypeStruct((cells, hd), BF16),
        in_specs=[
            any_spec, pl.BlockSpec(memory_space=pltpu.SMEM), any_spec, vmem,
            any_spec, any_spec, any_spec, vmem, vmem,
        ],
        out_specs=vmem,
        scratch_shapes=[
            pltpu.VMEM((rows, cols, chan), BF16),
            pltpu.VMEM((ext, cols, 128), BF16),
            pltpu.VMEM((rows // 2, 16, 128), BF16),
            pltpu.VMEM((rows // 2, 16, 128), BF16),
            pltpu.VMEM((pairs, 16, 128), BF16),
            pltpu.VMEM((pairs, 16, 128), BF16),
            pltpu.VMEM((chan, d), BF16),
            pltpu.VMEM((d, hd), BF16),
            pltpu.VMEM((d, hd), BF16),
            pltpu.VMEM((d, hd), BF16),
            pltpu.VMEM((256, 3 * hd + 128), BF16),
            pltpu.VMEM((256, 256), BF16),
            pltpu.VMEM((cells, hd), BF16),
            pltpu.VMEM((ext * cols, hd), BF16),
            pltpu.VMEM((ext * cols, hd), BF16),
            pltpu.VMEM((ext * SIDE, hd), BF16),
            pltpu.VMEM((ext * SIDE, hd), BF16),
            pltpu.VMEM((ext * SIDE, hd), BF16),
            pltpu.VMEM((ext * SIDE, hd), BF16),
            pltpu.VMEM((7, TR * cols, keys), BF16),
            pltpu.SemaphoreType.DMA((5,)),
            pltpu.SemaphoreType.DMA((8,)),
            pltpu.SemaphoreType.DMA((8,)),
        ],
        compiler_params=pltpu.CompilerParams(
            collective_id=0, has_side_effects=True, vmem_limit_bytes=48 * 1024 * 1024
        ),
    )(
        fields, row_valid, w_encode, norm_gain.reshape(1, d), w_query, w_key, w_value,
        query_gain.reshape(1, HEAD_DIM), key_gain.reshape(1, HEAD_DIM),
    )
    block = chunk_of(rows, 16)
    return pl.pallas_call(
        out_kernel,
        grid=(rows // block,),
        out_shape=jax.ShapeDtypeStruct((rows, cols, d), BF16),
        in_specs=[
            pl.BlockSpec((block, cols, chan), lambda i: (i, 0, 0)),
            pl.BlockSpec((chan, d), lambda i: (0, 0)),
            pl.BlockSpec((block * cols, hd), lambda i: (i, 0)),
            pl.BlockSpec((hd, d), lambda i: (0, 0)),
        ],
        out_specs=pl.BlockSpec((block, cols, d), lambda i: (i, 0, 0)),
        compiler_params=pltpu.CompilerParams(vmem_limit_bytes=32 * 1024 * 1024),
    )(fields, w_encode, mix, w_out)


def solution(mesh):
    return jax.shard_map(
        functools.partial(per_device, mesh.shape["lat"], mesh.shape["lon"]),
        mesh=mesh,
        in_specs=(P("lat", "lon", None), P("lat"), P(), P(), P(), P(), P(), P(), P(), P()),
        out_specs=P("lat", "lon", None),
        check_vma=False,
    )
```

time: 280 us -> 54.7 us (0.20)
  local copies, waits for them, and re-layouts: 143 us -> 8.84 us
  matrix products: 67.5 us -> 0 us
  Pallas kernels: 0 us -> 45.6 us
  other arithmetic: 27 us -> 0 us
  waiting for transfers between devices: 19.5 us -> 0 us
  starting transfers between devices: 17.5 us -> 0 us
  loops' own time: 2.94 us -> 0 us
    dot_general x13 -> x0, matrix products: 67.5 us -> none  [the longest x4 26.7 us: attend(): jnp.einsum('qhd,khd->hqk', qblock, kblock[:, 0], preferred_element_type=j...]
    pallas_call x0 -> x2, Pallas kernels: none -> 45.6 us  [the longest x1 39.6 us: per_device(): pl.pallas_call(functools.partial(attend_kernel, n_lat, n_lon, rows, cols,...]
    reshape x8 -> x0, local copies, waits for them, and re-layouts: 33.1 us -> none  [the longest x4 31 us: attend(): kblock = kblock.reshape(span_rows * span_cols, 2, HEADS, HEAD_DIM)]
    while x8 -> x0, local copies, waits for them, and re-layouts: 32.3 us -> none
    dynamic_slice x16 -> x0, local copies, waits for them, and re-layouts: 22.6 us -> none  [the longest x4 15.4 us: attend(): kblock = lax.dynamic_slice_in_dim(key_value, row_start, span_rows, 0)]
    slice x7 -> x0, local copies, waits for them, and re-layouts: 22.3 us -> none  [the longest x4 16.4 us: attend(): kblock[:, 1]]
    ppermute x4 -> x0, waiting for transfers between devices: 19.5 us -> none  [the longest x2 11.7 us: with_halo(): after = lax.ppermute(initial, axis, down)]
    ppermute x4 -> x0, starting transfers between devices: 17.5 us -> none  [the longest x2 13.3 us: with_halo(): after = lax.ppermute(initial, axis, down)]
  transfers between devices with their start and end apart: 4 -> 0, of which waited for: 4 -> 0; matrix products, arithmetic and copies ran while one was open for 11% -> 0% of each run, Pallas kernels for 0% -> 0%
where the time goes in v1:
time: 54.7 us; the launch traced here: 54.5 us
  Pallas kernels  45.6 us (83%)
  local copies, waits for them, and re-layouts  8.84 us (16%)
    pallas_call x1, Pallas kernels, per_device(): pl.pallas_call(functools.partial(attend_kernel, n_lat, n_lon, rows, cols,...  39.6 us
    unnamed x19, local copies, waits for them, and re-layouts  8.84 us
    pallas_call x1, Pallas kernels, per_device(): pl.pallas_call(out_kernel, grid=(rows // block,), out_shape=jax.ShapeDtyp...  5.94 us

profile of v1, /device:TPU:1, one launch (start us, length us, event | category | flops | bytes accessed | tf_op | source)
XLA Modules:
  0.0 54.5 jit_solution(8224155172437376324)
XLA Ops:
  0.0 0.0 copy-start
  0.0 1.6 %copy.12.fields = bf16[128,16,70]{2,1,0:T(8,128)(2,1)S(1)} copy(bf16[128,16,70]{0,1,2:T(8,128)(2,1)} %param.10) | data formatting | bytes 573440 | tf_op args[0]
  1.6 0.0 copy-start.1
  1.6 1.2 %copy-done.1 = bf16[1024,512]{1,0:T(8,128)(2,1)S(1)} copy-done((bf16[1024,512]{1,0:T(8,128)(2,1)S(1)}, bf16[1024,512]{1,0:T(8,128)(2,1)}, u32[]{:S(2)}) %copy-start.1) | copy-done | bytes 1048600
  2.9 0.0 copy-start.2
  2.9 1.2 %copy-done.2 = bf16[1024,512]{1,0:T(8,128)(2,1)S(1)} copy-done((bf16[1024,512]{1,0:T(8,128)(2,1)S(1)}, bf16[1024,512]{1,0:T(8,128)(2,1)}, u32[]{:S(2)}) %copy-start.2) | copy-done | bytes 1048600
  4.1 0.0 copy-start.3
  4.1 1.2 %copy-done.3 = bf16[1024,512]{1,0:T(8,128)(2,1)S(1)} copy-done((bf16[1024,512]{1,0:T(8,128)(2,1)S(1)}, bf16[1024,512]{1,0:T(8,128)(2,1)}, u32[]{:S(2)}) %copy-start.3) | copy-done | bytes 1048600
  5.3 0.0 copy-start.4
  5.3 0.9 %copy-done.4 = bf16[70,1024]{1,0:T(8,128)(2,1)S(1)} copy-done((bf16[70,1024]{1,0:T(8,128)(2,1)S(1)}, bf16[70,1024]{1,0:T(8,128)(2,1)}, u32[]{:S(2)}) %copy-start.4) | copy-done | bytes 143384
  6.2 0.0 copy-start.5
  6.2 0.7 %copy-done.5 = f32[1024]{0:T(1024)S(1)} copy-done((f32[1024]{0:T(1024)S(1)}, f32[1024]{0:T(1024)}, u32[]{:S(2)}) %copy-start.5) | copy-done | bytes 4120
  6.9 0.0 copy-start.6
  6.9 0.7 %copy-done.6 = s32[128]{0:T(128)S(1)} copy-done((s32[128]{0:T(128)S(1)}, s32[128]{0:T(128)}, u32[]{:S(2)}) %copy-start.6) | copy-done | bytes 536
  7.6 0.0 copy-start.7
  7.6 0.7 %copy-done.7 = f32[64]{0:T(128)S(1)} copy-done((f32[64]{0:T(128)S(1)}, f32[64]{0:T(128)}, u32[]{:S(2)}) %copy-start.7) | copy-done | bytes 280
  8.2 0.0 copy-start.8
  8.2 0.7 %copy-done.8 = f32[64]{0:T(128)S(1)} copy-done((f32[64]{0:T(128)S(1)}, f32[64]{0:T(128)}, u32[]{:S(2)}) %copy-start.8) | copy-done | bytes 280
  8.9 39.6 %shard_map.100.mix = bf16[2048,512]{1,0:T(8,128)(2,1)S(1)} custom-call(bf16[128,16,70]{2,1,0:T(8,128)(2,1)S(1)} %copy.12.fields, s32[128]{0:T(128)S(1)} %copy-done.6, bf16[70,1024]{1,0:T(8,128)(2,1)S(1)} %copy-done.4, f32[1,1024]{1,0:T(1,128)S(1)} %bitcast.3, bf16[1024,512]{1,0:T(8,128)(2,1)S(1)} %copy-done.1, bf16[1024,512]{1,0:T(8,128)(2,1)S(1)} %copy-done.2, ...), custom_call_target="tpu_custom_call" | custom-call | tf_op jit(solution)/shard_map/pallas_call | solution.py:264
  48.5 0.0 copy-done
  48.5 5.9 %shard_map.101 = bf16[128,16,1024]{2,1,0:T(8,128)(2,1)} custom-call(bf16[128,16,70]{2,1,0:T(8,128)(2,1)S(1)} %copy.12.fields, bf16[70,1024]{1,0:T(8,128)(2,1)S(1)} %copy-done.4, bf16[2048,512]{1,0:T(8,128)(2,1)S(1)} %shard_map.100.mix, bf16[512,1024]{1,0:T(8,128)(2,1)S(1)} %copy-done), custom_call_target="tpu_custom_call" | custom-call | tf_op jit(solution)/shard_map/pallas_call | solution.py:305
Async XLA Ops:
  0.0 48.5 %copy-start = (bf16[512,1024]{1,0:T(8,128)(2,1)S(1)}, bf16[512,1024]{1,0:T(8,128)(2,1)}, u32[]{:S(2)}) copy-start(bf16[512,1024]{1,0:T(8,128)(2,1)} %w_out.1) | copy-start | bytes 3145732
  1.6 1.2 %copy-start.1 = (bf16[1024,512]{1,0:T(8,128)(2,1)S(1)}, bf16[1024,512]{1,0:T(8,128)(2,1)}, u32[]{:S(2)}) copy-start(bf16[1024,512]{1,0:T(8,128)(2,1)} %w_q.1) | copy-start | bytes 3145732
  2.9 1.2 %copy-start.2 = (bf16[1024,512]{1,0:T(8,128)(2,1)S(1)}, bf16[1024,512]{1,0:T(8,128)(2,1)}, u32[]{:S(2)}) copy-start(bf16[1024,512]{1,0:T(8,128)(2,1)} %w_k.1) | copy-start | bytes 3145732
  4.1 1.2 %copy-start.3 = (bf16[1024,512]{1,0:T(8,128)(2,1)S(1)}, bf16[1024,512]{1,0:T(8,128)(2,1)}, u32[]{:S(2)}) copy-start(bf16[1024,512]{1,0:T(8,128)(2,1)} %w_v.1) | copy-start | bytes 3145732
  5.3 0.9 %copy-start.4 = (bf16[70,1024]{1,0:T(8,128)(2,1)S(1)}, bf16[70,1024]{1,0:T(8,128)(2,1)}, u32[]{:S(2)}) copy-start(bf16[70,1024]{1,0:T(8,128)(2,1)} %w_enc.3) | copy-start | bytes 430084
  6.2 0.7 %copy-start.5 = (f32[1024]{0:T(1024)S(1)}, f32[1024]{0:T(1024)}, u32[]{:S(2)}) copy-start(f32[1024]{0:T(1024)} %param.13) | copy-start | bytes 12292
  6.9 0.7 %copy-start.6 = (s32[128]{0:T(128)S(1)}, s32[128]{0:T(128)}, u32[]{:S(2)}) copy-start(s32[128]{0:T(128)} %valid.1) | copy-start | bytes 1540
  7.6 0.7 %copy-start.7 = (f32[64]{0:T(128)S(1)}, f32[64]{0:T(128)}, u32[]{:S(2)}) copy-start(f32[64]{0:T(128)} %param.17) | copy-start | bytes 772
  8.2 0.7 %copy-start.8 = (f32[64]{0:T(128)S(1)}, f32[64]{0:T(128)}, u32[]{:S(2)}) copy-start(f32[64]{0:T(128)} %param.18) | copy-start | bytes 772

commit v2 on v1

--- a/solution.py
+++ b/solution.py
@@ -40,9 +40,9 @@
 
 def attend_kernel(
     n_lat, n_lon, rows, cols, chan, hd,
-    fields, valid, w_enc, gain, w_q, w_k, w_v, q_gain, k_gain,
+    fields, row_valid, w_enc, norm_gain, w_q, w_k, w_v, query_gain, key_gain,
     mix,
-    fraw, fext, send_l, send_r, halo_l, halo_r, enc, wq, wk, wv, comp, ones_blk,
+    fraw, fext, send_l, send_r, halo_l, halo_r, enc, gain, wq, wk, wv, q_gain, k_gain, valid, comp, ones_blk,
     q_s, k_o, v_o, k_l, v_l, k_r, v_r, masks,
     local_sem, send_sem, recv_sem,
 ):
@@ -57,7 +57,10 @@
     loads = [
         pltpu.make_async_copy(src, dst, local_sem.at[i])
         for i, (src, dst) in enumerate(
-            ((fields, fraw), (w_enc, enc), (w_k, wk), (w_v, wv), (w_q, wq))
+            (
+                (fields, fraw), (w_enc, enc), (norm_gain, gain), (row_valid, valid), (query_gain, q_gain),
+                (key_gain, k_gain), (w_k, wk), (w_v, wv), (w_q, wq),
+            )
         )
     ]
     for load in loads:
@@ -126,6 +129,8 @@
     qi = lax.broadcasted_iota(jnp.int32, (TR * cols, 1), 0)
     row_off = key_row - qi // cols
     col_off = key_col - qi % cols
+    for load in loads[1:6]:
+        load.wait()
     near = (row_off >= 0) & (row_off <= 2 * HALO) & (col_off >= -HALO) & (col_off <= HALO)
     base = jnp.where(near, 1.0, 0.0).astype(F32)
     has_up = jnp.where(lat > 0, 1.0, 0.0).astype(F32)
@@ -146,7 +151,6 @@
             m = base * ok
         masks[slot] = m.astype(BF16)
 
-    loads[1].wait()
     enc_v = enc[...]
     wg_hi, wg_lo = split(enc_v.astype(F32) * gain[...])
 
@@ -156,7 +160,7 @@
         comp[128 : 128 + x.shape[0], at : at + x.shape[1]] = lo
 
     put(nt(enc_v, enc_v) * (1.0 / enc_v.shape[1]), 2 * hd)
-    for load, w, at in ((loads[2], wk, 0), (loads[3], wv, hd), (loads[4], wq, 2 * hd + 128)):
+    for load, w, at in ((loads[6], wk, 0), (loads[7], wv, hd), (loads[8], wq, 2 * hd + 128)):
         load.wait()
         put(nn(wg_hi, w[...]) + nn(wg_lo, w[...]), at)
 
@@ -194,7 +198,7 @@
         project(f, k_o, v_o, pl.multiple_of(HALO * cols + i * ccell, 16), pl.multiple_of(i * ccell, 16))
         return c
 
-    lax.fori_loop(0, rows // crow, own_step, 0)
+    lax.fori_loop(0, rows // crow, own_step, 0, unroll=8)
 
     for copy in copies:
         copy.wait_recv()
@@ -210,7 +214,7 @@
             project(f, k_ref, v_ref, pl.multiple_of(i * cpair * 16, 16))
         return c
 
-    lax.fori_loop(0, (pairs + 2 * hp) // cpair, side_step, 0)
+    lax.fori_loop(0, (pairs + 2 * hp) // cpair, side_step, 0, unroll=5)
 
     nq = TR * cols
     head = lax.broadcasted_iota(jnp.int32, (nq, 256), 1) // HEAD_DIM
@@ -238,7 +242,7 @@
             mix[q_at, ps] = out.astype(BF16)
         return c
 
-    lax.fori_loop(0, tiles, attend, 0, unroll=2)
+    lax.fori_loop(0, tiles, attend, 0, unroll=8)
 
     for copy in copies:
         copy.wait_send()
@@ -258,16 +262,13 @@
     cells = rows * cols
     ext = rows + 2 * HALO
     pairs = ext // 2
-    any_spec = pl.BlockSpec(memory_space=pl.ANY)
+    hbm = pl.BlockSpec(memory_space=pltpu.HBM)
     vmem = pl.BlockSpec(memory_space=pltpu.VMEM)
     keys = (TR + 2 * HALO) * (cols + 2 * SIDE)
     mix = pl.pallas_call(
         functools.partial(attend_kernel, n_lat, n_lon, rows, cols, chan, hd),
         out_shape=jax.ShapeDtypeStruct((cells, hd), BF16),
-        in_specs=[
-            any_spec, pl.BlockSpec(memory_space=pltpu.SMEM), any_spec, vmem,
-            any_spec, any_spec, any_spec, vmem, vmem,
-        ],
+        in_specs=[hbm] * 9,
         out_specs=vmem,
         scratch_shapes=[
             pltpu.VMEM((rows, cols, chan), BF16),
@@ -277,9 +278,13 @@
             pltpu.VMEM((pairs, 16, 128), BF16),
             pltpu.VMEM((pairs, 16, 128), BF16),
             pltpu.VMEM((chan, d), BF16),
+            pltpu.VMEM((1, d), F32),
             pltpu.VMEM((d, hd), BF16),
             pltpu.VMEM((d, hd), BF16),
             pltpu.VMEM((d, hd), BF16),
+            pltpu.VMEM((1, HEAD_DIM), F32),
+            pltpu.VMEM((1, HEAD_DIM), F32),
+            pltpu.SMEM((rows,), jnp.int32),
             pltpu.VMEM((256, 3 * hd + 128), BF16),
             pltpu.VMEM((256, 256), BF16),
             pltpu.VMEM((cells, hd), BF16),
@@ -290,12 +295,12 @@
             pltpu.VMEM((ext * SIDE, hd), BF16),
             pltpu.VMEM((ext * SIDE, hd), BF16),
             pltpu.VMEM((7, TR * cols, keys), BF16),
-            pltpu.SemaphoreType.DMA((5,)),
+            pltpu.SemaphoreType.DMA((9,)),
             pltpu.SemaphoreType.DMA((8,)),
             pltpu.SemaphoreType.DMA((8,)),
         ],
         compiler_params=pltpu.CompilerParams(
-            collective_id=0, has_side_effects=True, vmem_limit_bytes=48 * 1024 * 1024
+            collective_id=0, has_side_effects=True, vmem_limit_bytes=63 * 1024 * 1024
         ),
     )(
         fields, row_valid, w_encode, norm_gain.reshape(1, d), w_query, w_key, w_value,
@@ -313,7 +318,7 @@
             pl.BlockSpec((hd, d), lambda i: (0, 0)),
         ],
         out_specs=pl.BlockSpec((block, cols, d), lambda i: (i, 0, 0)),
-        compiler_params=pltpu.CompilerParams(vmem_limit_bytes=32 * 1024 * 1024),
+        compiler_params=pltpu.CompilerParams(vmem_limit_bytes=63 * 1024 * 1024),
     )(fields, w_encode, mix, w_out)
 
 

time: 54.7 us -> 46.7 us (0.85)
  local copies, waits for them, and re-layouts: 8.84 us -> 2.29 us
  Pallas kernels: 45.6 us -> 44.1 us
    unnamed x19 -> x1, local copies, waits for them, and re-layouts: 8.84 us -> 2.29 us
    pallas_call x1, Pallas kernels: 39.6 us -> 35.4 us  [per_device(): pl.pallas_call(functools.partial(attend_kernel, n_lat, n_lon, rows, cols,...]
    pallas_call x1, Pallas kernels: 5.94 us -> 8.64 us  [per_device(): pl.pallas_call(out_kernel, grid=(rows // block,), out_shape=jax.ShapeDtyp...]
where the time goes in v2:
time: 46.7 us; the launch traced here: 46.4 us
  Pallas kernels  44.1 us (94%)
  local copies, waits for them, and re-layouts  2.29 us (5%)
    pallas_call x1, Pallas kernels, per_device(): pl.pallas_call(functools.partial(attend_kernel, n_lat, n_lon, rows, cols,...  35.4 us
    pallas_call x1, Pallas kernels, per_device(): pl.pallas_call(out_kernel, grid=(rows // block,), out_shape=jax.ShapeDtyp...  8.64 us
    unnamed x1, local copies, waits for them, and re-layouts  2.29 us

profile of v2, /device:TPU:1, one launch (start us, length us, event | category | flops | bytes accessed | tf_op | source)
XLA Modules:
  0.0 46.4 jit_solution(10229685520224162444)
XLA Ops:
  0.0 2.3 %copy.12.fields = bf16[128,16,70]{2,1,0:T(8,128)(2,1)} copy(bf16[128,16,70]{0,1,2:T(8,128)(2,1)} %param.10) | data formatting | bytes 573440 | tf_op args[0]
  2.3 35.4 %shard_map.100.mix = bf16[2048,512]{1,0:T(8,128)(2,1)} custom-call(bf16[128,16,70]{2,1,0:T(8,128)(2,1)} %copy.12.fields, s32[128]{0:T(128)} %row_valid.1, bf16[70,1024]{1,0:T(8,128)(2,1)} %w_enc.3, f32[1,1024]{1,0:T(1,128)} %bitcast.3, bf16[1024,512]{1,0:T(8,128)(2,1)} %w_q.1, bf16[1024,512]{1,0:T(8,128)(2,1)} %w_k.1, bf16[1024,512]{1,0:T(8,128)(2,1)} %w_v.1, ...), custom_call_target="tpu_custom_call" | custom-call | tf_op jit(solution)/shard_map/pallas_call | solution.py:268
  37.7 8.6 %shard_map.101 = bf16[128,16,1024]{2,1,0:T(8,128)(2,1)} custom-call(bf16[128,16,70]{2,1,0:T(8,128)(2,1)} %copy.12.fields, bf16[70,1024]{1,0:T(8,128)(2,1)} %w_enc.3, bf16[2048,512]{1,0:T(8,128)(2,1)} %shard_map.100.mix, bf16[512,1024]{1,0:T(8,128)(2,1)} %w_out.1), custom_call_target="tpu_custom_call" | custom-call | tf_op jit(solution)/shard_map/pallas_call | solution.py:310

commit v3 on v2

--- a/solution.py
+++ b/solution.py
@@ -42,7 +42,7 @@
     n_lat, n_lon, rows, cols, chan, hd,
     fields, row_valid, w_enc, norm_gain, w_q, w_k, w_v, query_gain, key_gain,
     mix,
-    fraw, fext, send_l, send_r, halo_l, halo_r, enc, gain, wq, wk, wv, q_gain, k_gain, valid, comp, ones_blk,
+    num_s, den_s, fraw, fext, send_l, send_r, halo_l, halo_r, enc, gain, wq, wk, wv, q_gain, k_gain, valid, comp, ones_blk,
     q_s, k_o, v_o, k_l, v_l, k_r, v_r, masks,
     local_sem, send_sem, recv_sem,
 ):
@@ -200,11 +200,56 @@
 
     lax.fori_loop(0, rows // crow, own_step, 0, unroll=8)
 
+    nq = TR * cols
+    head = lax.broadcasted_iota(jnp.int32, (nq, 256), 1) // HEAD_DIM
+
+    def pick(x):
+        y = x[0:nq]
+        for h in range(1, 4):
+            y = jnp.where(head == h, x[h * nq : (h + 1) * nq], y)
+        return y
+
+    def partial(t, p, k, v, lanes):
+        ps = slice(256 * p, 256 * p + 256)
+        q_at = pl.ds(pl.multiple_of(t * nq, nq), nq)
+        slot = jnp.minimum(t, 3) + jnp.maximum(t - (tiles - 4), 0)
+        q = q_s[q_at, ps]
+        zero = jnp.zeros_like(q)
+        q4 = jnp.concatenate([jnp.where(head == h, q, zero) for h in range(4)], axis=0)
+        m = masks[slot, :, lanes]
+        e = jnp.exp2(nt(q4, k)).astype(BF16) * jnp.concatenate([m] * 4, axis=0)
+        den = jnp.sum(e.astype(F32), axis=1, keepdims=True)
+        return q_at, ps, pick(nn(e, v)), pick(den)
+
+    def own_part(t, c):
+        o_at = pl.ds(pl.multiple_of(t * nq, nq), half)
+        for p in range(hd // 256):
+            ps = slice(256 * p, 256 * p + 256)
+            q_at, ps, num, den = partial(t, p, k_o[o_at, ps], v_o[o_at, ps], slice(0, half))
+            num_s[q_at, ps] = num
+            den_s[q_at, ps] = den
+        return c
+
+    def side_part(t, c):
+        s_at = pl.ds(pl.multiple_of(t * TR * SIDE, TR * SIDE), side)
+        for p in range(hd // 256):
+            ps = slice(256 * p, 256 * p + 256)
+            k = jnp.concatenate([k_l[s_at, ps], k_r[s_at, ps]], axis=0)
+            v = jnp.concatenate([v_l[s_at, ps], v_r[s_at, ps]], axis=0)
+            q_at, ps, num, den = partial(t, p, k, v, slice(half, keys))
+            mix[q_at, ps] = ((num_s[q_at, ps] + num) / (den_s[q_at, ps] + den)).astype(BF16)
+        return c
+
+    edge = -(-HALO // TR)
+    lax.fori_loop(edge, tiles - edge, own_part, 0, unroll=chunk_of(tiles - 2 * edge, 7))
+
     for copy in copies:
         copy.wait_recv()
 
     for r0 in (0, HALO + rows):
         project(fext[r0 : r0 + HALO].reshape(HALO * cols, 128), k_o, v_o, r0 * cols)
+    for t in (*range(edge), *range(tiles - edge, tiles)):
+        own_part(t, 0)
 
     cpair = chunk_of(pairs + 2 * hp, 14)
 
@@ -216,33 +261,7 @@
 
     lax.fori_loop(0, (pairs + 2 * hp) // cpair, side_step, 0, unroll=5)
 
-    nq = TR * cols
-    head = lax.broadcasted_iota(jnp.int32, (nq, 256), 1) // HEAD_DIM
-
-    def attend(t, c):
-        slot = jnp.minimum(t, 3) + jnp.maximum(t - (tiles - 4), 0)
-        m = masks[slot]
-        m4 = jnp.concatenate([m] * 4, axis=0)
-        o_at = pl.ds(pl.multiple_of(t * nq, nq), half)
-        s_at = pl.ds(pl.multiple_of(t * TR * SIDE, TR * SIDE), side)
-        q_at = pl.ds(pl.multiple_of(t * nq, nq), nq)
-        for p in range(hd // 256):
-            ps = slice(256 * p, 256 * p + 256)
-            q = q_s[q_at, ps]
-            zero = jnp.zeros_like(q)
-            q4 = jnp.concatenate([jnp.where(head == h, q, zero) for h in range(4)], axis=0)
-            k = jnp.concatenate([k_o[o_at, ps], k_l[s_at, ps], k_r[s_at, ps]], axis=0)
-            v = jnp.concatenate([v_o[o_at, ps], v_l[s_at, ps], v_r[s_at, ps]], axis=0)
-            e = jnp.exp2(nt(q4, k)).astype(BF16) * m4
-            den = jnp.sum(e.astype(F32), axis=1, keepdims=True)
-            acc = nn(e, v) * (1.0 / den)
-            out = acc[0:nq]
-            for h in range(1, 4):
-                out = jnp.where(head == h, acc[h * nq : (h + 1) * nq], out)
-            mix[q_at, ps] = out.astype(BF16)
-        return c
-
-    lax.fori_loop(0, tiles, attend, 0, unroll=8)
+    lax.fori_loop(0, tiles, side_part, 0, unroll=8)
 
     for copy in copies:
         copy.wait_send()
@@ -271,6 +290,8 @@
         in_specs=[hbm] * 9,
         out_specs=vmem,
         scratch_shapes=[
+            pltpu.VMEM((cells, hd), F32),
+            pltpu.VMEM((cells, hd), F32),
             pltpu.VMEM((rows, cols, chan), BF16),
             pltpu.VMEM((ext, cols, 128), BF16),
             pltpu.VMEM((rows // 2, 16, 128), BF16),
@@ -306,7 +327,7 @@
         fields, row_valid, w_encode, norm_gain.reshape(1, d), w_query, w_key, w_value,
         query_gain.reshape(1, HEAD_DIM), key_gain.reshape(1, HEAD_DIM),
     )
-    block = chunk_of(rows, 16)
+    block = chunk_of(rows, 32)
     return pl.pallas_call(
         out_kernel,
         grid=(rows // block,),

time: 46.7 us -> 44.5 us (0.953)
  Pallas kernels: 44.1 us -> 42 us
    pallas_call x1, Pallas kernels: 8.64 us -> 6.94 us  [per_device(): pl.pallas_call(out_kernel, grid=(rows // block,), out_shape=jax.ShapeDtyp...]
where the time goes in v3:
time: 44.5 us; the launch traced here: 44.3 us
  Pallas kernels  42 us (94%)
  local copies, waits for them, and re-layouts  2.29 us (5%)
    pallas_call x1, Pallas kernels, per_device(): pl.pallas_call(functools.partial(attend_kernel, n_lat, n_lon, rows, cols,...  35.1 us
    pallas_call x1, Pallas kernels, per_device(): pl.pallas_call(out_kernel, grid=(rows // block,), out_shape=jax.ShapeDtyp...  6.94 us
    unnamed x1, local copies, waits for them, and re-layouts  2.29 us

profile of v3, /device:TPU:1, one launch (start us, length us, event | category | flops | bytes accessed | tf_op | source)
XLA Modules:
  0.0 44.3 jit_solution(3452210871509661388)
XLA Ops:
  0.0 2.3 %copy.12.fields = bf16[128,16,70]{2,1,0:T(8,128)(2,1)} copy(bf16[128,16,70]{0,1,2:T(8,128)(2,1)} %param.10) | data formatting | bytes 573440 | tf_op args[0]
  2.3 35.1 %shard_map.100.mix = bf16[2048,512]{1,0:T(8,128)(2,1)} custom-call(bf16[128,16,70]{2,1,0:T(8,128)(2,1)} %copy.12.fields, s32[128]{0:T(128)} %row_valid.1, bf16[70,1024]{1,0:T(8,128)(2,1)} %w_enc.3, f32[1,1024]{1,0:T(1,128)} %bitcast.3, bf16[1024,512]{1,0:T(8,128)(2,1)} %w_q.1, bf16[1024,512]{1,0:T(8,128)(2,1)} %w_k.1, bf16[1024,512]{1,0:T(8,128)(2,1)} %w_v.1, ...), custom_call_target="tpu_custom_call" | custom-call | tf_op jit(solution)/shard_map/pallas_call | solution.py:287
  37.4 6.9 %shard_map.101 = bf16[128,16,1024]{2,1,0:T(8,128)(2,1)} custom-call(bf16[128,16,70]{2,1,0:T(8,128)(2,1)} %copy.12.fields, bf16[70,1024]{1,0:T(8,128)(2,1)} %w_enc.3, bf16[2048,512]{1,0:T(8,128)(2,1)} %shard_map.100.mix, bf16[512,1024]{1,0:T(8,128)(2,1)} %w_out.1), custom_call_target="tpu_custom_call" | custom-call | tf_op jit(solution)/shard_map/pallas_call | solution.py:331

commit v4 on v3

--- a/solution.py
+++ b/solution.py
@@ -13,6 +13,7 @@
 HALO = 6
 TR = 4
 SIDE = 8
+RING = 8
 EPS_ROW = 1e-05
 EPS_HEAD = 1e-06
 F32 = jnp.float32
@@ -40,25 +41,23 @@
 
 def attend_kernel(
     n_lat, n_lon, rows, cols, chan, hd,
-    fields, row_valid, w_enc, norm_gain, w_q, w_k, w_v, query_gain, key_gain,
+    fields, fields_t, row_valid, w_enc, norm_gain, w_q, w_k, w_v, query_gain, key_gain,
     mix,
-    num_s, den_s, fraw, fext, send_l, send_r, halo_l, halo_r, enc, gain, wq, wk, wv, q_gain, k_gain, valid, comp, ones_blk,
+    num_s, den_s, ft, work, x_l, x_r, c_ul, c_ur, c_dl, c_dr, fraw, fext, send_l, send_r, halo_l, halo_r, enc, gain, wq, wk, wv, q_gain, k_gain, valid, comp, ones_blk,
     q_s, k_o, v_o, k_l, v_l, k_r, v_r, masks,
     local_sem, send_sem, recv_sem,
 ):
     lat, lon = lax.axis_index("lat"), lax.axis_index("lon")
     up, down = lax.rem(lat + n_lat - 1, n_lat), lax.rem(lat + 1, n_lat)
     left, right = lax.rem(lon + n_lon - 1, n_lon), lax.rem(lon + 1, n_lon)
-    pairs = rows // 2
     ext = rows + 2 * HALO
     tiles = rows // TR
-    hp = HALO // 2
 
     loads = [
         pltpu.make_async_copy(src, dst, local_sem.at[i])
         for i, (src, dst) in enumerate(
             (
-                (fields, fraw), (w_enc, enc), (norm_gain, gain), (row_valid, valid), (query_gain, q_gain),
+                (fields, fraw), (fields_t, ft), (w_enc, enc), (norm_gain, gain), (row_valid, valid), (query_gain, q_gain),
                 (key_gain, k_gain), (w_k, wk), (w_v, wv), (w_q, wq),
             )
         )
@@ -73,34 +72,29 @@
     for dev in around:
         pl.semaphore_signal(barrier, inc=1, device_id=dev, device_id_type=MESH)
 
-    own = pl.ds(HALO, rows)
-    fext[own] = jnp.zeros((rows, cols, 128), BF16)
-    send_l[...] = jnp.zeros(send_l.shape, BF16)
-    send_r[...] = jnp.zeros(send_r.shape, BF16)
-    loads[0].wait()
+    half_chan = chan // 2
+    step = chunk_of(half_chan, 7)
+    loads[1].wait()
 
     def pack(i, c):
-        x = fraw[pl.ds(i * 8, 8)]
-        fext[pl.ds(HALO + i * 8, 8), :, 0:chan] = x
-        x = x.astype(F32)
-        send_l[pl.ds(i * 4, 4), :, 0:chan] = x[:, 0:SIDE].reshape(4, 16, chan).astype(BF16)
-        send_r[pl.ds(i * 4, 4), :, 0:chan] = x[:, cols - SIDE :].reshape(4, 16, chan).astype(BF16)
-        return c
-
-    lax.fori_loop(0, rows // 8, pack, 0)
-    pl.semaphore_wait(barrier, 8)
-
-    first, last = pl.ds(0, hp), pl.ds(pairs - hp, hp)
-    top, mid, bot = pl.ds(0, hp), pl.ds(hp, pairs), pl.ds(hp + pairs, hp)
+        x = ft[pl.ds(i * 2 * step, 2 * step)].astype(F32)
+        send_l[pl.ds(i * step, step)] = x[:, 0:SIDE].reshape(step, 16, rows).astype(BF16)
+        send_r[pl.ds(i * step, step)] = x[:, cols - SIDE :].reshape(step, 16, rows).astype(BF16)
+        return c
+
+    lax.fori_loop(0, half_chan // step, pack, 0)
+
+    head_rows, tail_rows = pl.ds(HALO, HALO), pl.ds(rows, HALO)
+    above, below = pl.ds(0, HALO), pl.ds(HALO + rows, HALO)
     plan = [
-        (send_l.at[...], halo_r.at[mid], (lat, left)),
-        (send_r.at[...], halo_l.at[mid], (lat, right)),
-        (fext.at[pl.ds(HALO, HALO)], fext.at[pl.ds(HALO + rows, HALO)], (up, lon)),
-        (fext.at[pl.ds(rows, HALO)], fext.at[pl.ds(0, HALO)], (down, lon)),
-        (send_l.at[first], halo_r.at[bot], (up, left)),
-        (send_l.at[last], halo_r.at[top], (down, left)),
-        (send_r.at[first], halo_l.at[bot], (up, right)),
-        (send_r.at[last], halo_l.at[top], (down, right)),
+        (send_l.at[...], halo_r.at[...], (lat, left)),
+        (send_r.at[...], halo_l.at[...], (lat, right)),
+        (fext.at[head_rows], fext.at[below], (up, lon)),
+        (fext.at[tail_rows], fext.at[above], (down, lon)),
+        (fext.at[head_rows], c_dr.at[...], (up, left)),
+        (fext.at[tail_rows], c_ur.at[...], (down, left)),
+        (fext.at[head_rows], c_dl.at[...], (up, right)),
+        (fext.at[tail_rows], c_ul.at[...], (down, right)),
     ]
     copies = [
         pltpu.make_async_remote_copy(
@@ -109,8 +103,28 @@
         )
         for i, (src, dst, dev) in enumerate(plan)
     ]
-    for copy in copies:
-        copy.start()
+
+    early = lax.rem(lon, RING) == 0
+
+    def meet():
+        pl.semaphore_wait(barrier, 8)
+        for copy in copies[:2]:
+            copy.start()
+
+    @pl.when(jnp.logical_not(early))
+    def _():
+        meet()
+
+    fext[pl.ds(HALO, rows)] = jnp.zeros((rows, cols, 128), BF16)
+    loads[0].wait()
+    fext[pl.ds(HALO, rows), :, 0:chan] = fraw[...]
+
+    @pl.when(jnp.logical_not(early))
+    def _():
+        for copy in copies[2:]:
+            copy.start()
+
+    work[...] = jnp.zeros(work.shape, F32)
 
     comp[...] = jnp.zeros(comp.shape, BF16)
     row_i = lax.broadcasted_iota(jnp.int32, (256, 256), 0) // HEAD_DIM
@@ -129,7 +143,7 @@
     qi = lax.broadcasted_iota(jnp.int32, (TR * cols, 1), 0)
     row_off = key_row - qi // cols
     col_off = key_col - qi % cols
-    for load in loads[1:6]:
+    for load in loads[2:7]:
         load.wait()
     near = (row_off >= 0) & (row_off <= 2 * HALO) & (col_off >= -HALO) & (col_off <= HALO)
     base = jnp.where(near, 1.0, 0.0).astype(F32)
@@ -160,7 +174,7 @@
         comp[128 : 128 + x.shape[0], at : at + x.shape[1]] = lo
 
     put(nt(enc_v, enc_v) * (1.0 / enc_v.shape[1]), 2 * hd)
-    for load, w, at in ((loads[6], wk, 0), (loads[7], wv, hd), (loads[8], wq, 2 * hd + 128)):
+    for load, w, at in ((loads[7], wk, 0), (loads[8], wv, hd), (loads[9], wq, 2 * hd + 128)):
         load.wait()
         put(nn(wg_hi, w[...]) + nn(wg_lo, w[...]), at)
 
@@ -200,6 +214,12 @@
 
     lax.fori_loop(0, rows // crow, own_step, 0, unroll=8)
 
+    @pl.when(early)
+    def _():
+        meet()
+        for copy in copies[2:]:
+            copy.start()
+
     nq = TR * cols
     head = lax.broadcasted_iota(jnp.int32, (nq, 256), 1) // HEAD_DIM
 
@@ -251,15 +271,26 @@
     for t in (*range(edge), *range(tiles - edge, tiles)):
         own_part(t, 0)
 
-    cpair = chunk_of(pairs + 2 * hp, 14)
+    lead = HALO * SIDE
+    for halo, x_ref, up_ref, down_ref, at in (
+        (halo_l, x_l, c_ul, c_dl, cols - SIDE), (halo_r, x_r, c_ur, c_dr, 0)
+    ):
+        work[0 : chan * SIDE, :] = halo[...].astype(F32).reshape(chan * SIDE, rows)
+        x_ref[0:lead, :] = up_ref[...].astype(F32)[:, at : at + SIDE].reshape(lead, 128)
+        x_ref[lead + rows * SIDE :, :] = down_ref[...].astype(F32)[:, at : at + SIDE].reshape(lead, 128)
+        for c in range(SIDE):
+            block = work[pl.ds(c, 128, stride=SIDE), :]
+            x_ref[pl.ds(lead + c, rows, stride=SIDE), :] = block.T
+
+    cside = chunk_of(ext // 2, 14) * 2 * SIDE
 
     def side_step(i, c):
-        for src, k_ref, v_ref in ((halo_l, k_l, v_l), (halo_r, k_r, v_r)):
-            f = src[pl.ds(i * cpair, cpair)].reshape(cpair * 16, 128)
-            project(f, k_ref, v_ref, pl.multiple_of(i * cpair * 16, 16))
-        return c
-
-    lax.fori_loop(0, (pairs + 2 * hp) // cpair, side_step, 0, unroll=5)
+        for x_ref, k_ref, v_ref in ((x_l, k_l, v_l), (x_r, k_r, v_r)):
+            at = pl.multiple_of(i * cside, 16)
+            project(x_ref[pl.ds(at, cside), :].astype(BF16), k_ref, v_ref, at)
+        return c
+
+    lax.fori_loop(0, ext * SIDE // cside, side_step, 0, unroll=5)
 
     lax.fori_loop(0, tiles, side_part, 0, unroll=8)
 
@@ -280,24 +311,32 @@
     d, hd = w_query.shape
     cells = rows * cols
     ext = rows + 2 * HALO
-    pairs = ext // 2
+    fields_t = jnp.transpose(fields, (2, 1, 0))
     hbm = pl.BlockSpec(memory_space=pltpu.HBM)
     vmem = pl.BlockSpec(memory_space=pltpu.VMEM)
     keys = (TR + 2 * HALO) * (cols + 2 * SIDE)
     mix = pl.pallas_call(
         functools.partial(attend_kernel, n_lat, n_lon, rows, cols, chan, hd),
         out_shape=jax.ShapeDtypeStruct((cells, hd), BF16),
-        in_specs=[hbm] * 9,
+        in_specs=[hbm] * 10,
         out_specs=vmem,
         scratch_shapes=[
             pltpu.VMEM((cells, hd), F32),
             pltpu.VMEM((cells, hd), F32),
+            pltpu.VMEM((chan, cols, rows), BF16),
+            pltpu.VMEM((128 * SIDE, rows), F32),
+            pltpu.VMEM((ext * SIDE, 128), F32),
+            pltpu.VMEM((ext * SIDE, 128), F32),
+            pltpu.VMEM((HALO, cols, 128), BF16),
+            pltpu.VMEM((HALO, cols, 128), BF16),
+            pltpu.VMEM((HALO, cols, 128), BF16),
+            pltpu.VMEM((HALO, cols, 128), BF16),
             pltpu.VMEM((rows, cols, chan), BF16),
             pltpu.VMEM((ext, cols, 128), BF16),
-            pltpu.VMEM((rows // 2, 16, 128), BF16),
-            pltpu.VMEM((rows // 2, 16, 128), BF16),
-            pltpu.VMEM((pairs, 16, 128), BF16),
-            pltpu.VMEM((pairs, 16, 128), BF16),
+            pltpu.VMEM((chan // 2, 16, rows), BF16),
+            pltpu.VMEM((chan // 2, 16, rows), BF16),
+            pltpu.VMEM((chan // 2, 16, rows), BF16),
+            pltpu.VMEM((chan // 2, 16, rows), BF16),
             pltpu.VMEM((chan, d), BF16),
             pltpu.VMEM((1, d), F32),
             pltpu.VMEM((d, hd), BF16),
@@ -316,7 +355,7 @@
             pltpu.VMEM((ext * SIDE, hd), BF16),
             pltpu.VMEM((ext * SIDE, hd), BF16),
             pltpu.VMEM((7, TR * cols, keys), BF16),
-            pltpu.SemaphoreType.DMA((9,)),
+            pltpu.SemaphoreType.DMA((10,)),
             pltpu.SemaphoreType.DMA((8,)),
             pltpu.SemaphoreType.DMA((8,)),
         ],
@@ -324,7 +363,7 @@
             collective_id=0, has_side_effects=True, vmem_limit_bytes=63 * 1024 * 1024
         ),
     )(
-        fields, row_valid, w_encode, norm_gain.reshape(1, d), w_query, w_key, w_value,
+        fields, fields_t, row_valid, w_encode, norm_gain.reshape(1, d), w_query, w_key, w_value,
         query_gain.reshape(1, HEAD_DIM), key_gain.reshape(1, HEAD_DIM),
     )
     block = chunk_of(rows, 32)

time: 44.5 us -> 40.4 us (0.908)
  Pallas kernels: 42 us -> 37.9 us
    pallas_call x1, Pallas kernels: 35.1 us -> 30.9 us  [per_device(): pl.pallas_call(functools.partial(attend_kernel, n_lat, n_lon, rows, cols,...]
where the time goes in v4:
time: 40.4 us; the launch traced here: 40.2 us
  Pallas kernels  37.9 us (94%)
  local copies, waits for them, and re-layouts  2.29 us (6%)
    pallas_call x1, Pallas kernels, per_device(): pl.pallas_call(functools.partial(attend_kernel, n_lat, n_lon, rows, cols,...  30.9 us
    pallas_call x1, Pallas kernels, per_device(): pl.pallas_call(out_kernel, grid=(rows // block,), out_shape=jax.ShapeDtyp...  6.93 us
    unnamed x1, local copies, waits for them, and re-layouts  2.29 us

profile of v4, /device:TPU:1, one launch (start us, length us, event | category | flops | bytes accessed | tf_op | source)
XLA Modules:
  0.0 40.2 jit_solution(17482158262027365370)
XLA Ops:
  0.0 2.3 %copy.12.fields = bf16[128,16,70]{2,1,0:T(8,128)(2,1)} copy(bf16[128,16,70]{0,1,2:T(8,128)(2,1)} %param.10) | data formatting | bytes 573440 | tf_op args[0]
  2.3 30.9 %shard_map.100.mix = bf16[2048,512]{1,0:T(8,128)(2,1)} custom-call(bf16[128,16,70]{2,1,0:T(8,128)(2,1)} %copy.12.fields, bf16[70,16,128]{2,1,0:T(8,128)(2,1)} %bitcast.4, s32[128]{0:T(128)} %row_valid.1, bf16[70,1024]{1,0:T(8,128)(2,1)} %w_enc.3, f32[1,1024]{1,0:T(1,128)} %bitcast.5, bf16[1024,512]{1,0:T(8,128)(2,1)} %w_q.1, bf16[1024,512]{1,0:T(8,128)(2,1)} %w_k.1, ...), custom_call_target="tpu_custom_call" | custom-call | tf_op jit(solution)/shard_map/pallas_call | solution.py:318
  33.2 6.9 %shard_map.101 = bf16[128,16,1024]{2,1,0:T(8,128)(2,1)} custom-call(bf16[128,16,70]{2,1,0:T(8,128)(2,1)} %copy.12.fields, bf16[70,1024]{1,0:T(8,128)(2,1)} %w_enc.3, bf16[2048,512]{1,0:T(8,128)(2,1)} %shard_map.100.mix, bf16[512,1024]{1,0:T(8,128)(2,1)} %w_out.1), custom_call_target="tpu_custom_call" | custom-call | tf_op jit(solution)/shard_map/pallas_call | solution.py:370

commit v5 on v4

--- a/solution.py
+++ b/solution.py
@@ -41,11 +41,11 @@
 
 def attend_kernel(
     n_lat, n_lon, rows, cols, chan, hd,
-    fields, fields_t, row_valid, w_enc, norm_gain, w_q, w_k, w_v, query_gain, key_gain,
-    mix,
-    num_s, den_s, ft, work, x_l, x_r, c_ul, c_ur, c_dl, c_dr, fraw, fext, send_l, send_r, halo_l, halo_r, enc, gain, wq, wk, wv, q_gain, k_gain, valid, comp, ones_blk,
+    fields_t, row_valid, w_enc, norm_gain, w_q, w_k, w_v, query_gain, key_gain,
+    mix, cells_out,
+    num_s, den_s, ft, work, cell_f, x_l, x_r, c_ul, c_ur, c_dl, c_dr, fext, send_l, send_r, halo_l, halo_r, enc, gain, wq, wk, wv, q_gain, k_gain, valid, comp, ones_blk,
     q_s, k_o, v_o, k_l, v_l, k_r, v_r, masks,
-    local_sem, send_sem, recv_sem,
+    local_sem, send_sem, recv_sem, out_sem,
 ):
     lat, lon = lax.axis_index("lat"), lax.axis_index("lon")
     up, down = lax.rem(lat + n_lat - 1, n_lat), lax.rem(lat + 1, n_lat)
@@ -57,7 +57,7 @@
         pltpu.make_async_copy(src, dst, local_sem.at[i])
         for i, (src, dst) in enumerate(
             (
-                (fields, fraw), (fields_t, ft), (w_enc, enc), (norm_gain, gain), (row_valid, valid), (query_gain, q_gain),
+                (fields_t, ft), (w_enc, enc), (norm_gain, gain), (row_valid, valid), (query_gain, q_gain),
                 (key_gain, k_gain), (w_k, wk), (w_v, wv), (w_q, wq),
             )
         )
@@ -72,17 +72,15 @@
     for dev in around:
         pl.semaphore_signal(barrier, inc=1, device_id=dev, device_id_type=MESH)
 
-    half_chan = chan // 2
-    step = chunk_of(half_chan, 7)
-    loads[1].wait()
-
-    def pack(i, c):
-        x = ft[pl.ds(i * 2 * step, 2 * step)].astype(F32)
-        send_l[pl.ds(i * step, step)] = x[:, 0:SIDE].reshape(step, 16, rows).astype(BF16)
-        send_r[pl.ds(i * step, step)] = x[:, cols - SIDE :].reshape(step, 16, rows).astype(BF16)
-        return c
-
-    lax.fori_loop(0, half_chan // step, pack, 0)
+    work[chan * cols :, :] = jnp.zeros((work.shape[0] - chan * cols, rows), F32)
+    x_l[...] = jnp.zeros(x_l.shape, F32)
+    x_r[...] = jnp.zeros(x_r.shape, F32)
+    loads[0].wait()
+    work[0 : chan * cols, :] = ft[...].astype(F32).reshape(chan * cols, rows)
+    deep = send_l.shape[1]
+    for c in range(HALO):
+        send_l[c] = work[pl.ds(c, deep, stride=cols), :].astype(BF16)
+        send_r[c] = work[pl.ds(cols - HALO + c, deep, stride=cols), :].astype(BF16)
 
     head_rows, tail_rows = pl.ds(HALO, HALO), pl.ds(rows, HALO)
     above, below = pl.ds(0, HALO), pl.ds(HALO + rows, HALO)
@@ -115,16 +113,16 @@
     def _():
         meet()
 
-    fext[pl.ds(HALO, rows)] = jnp.zeros((rows, cols, 128), BF16)
-    loads[0].wait()
-    fext[pl.ds(HALO, rows), :, 0:chan] = fraw[...]
+    for c in range(cols):
+        cell_f[pl.ds(c, rows, stride=cols), :] = work[pl.ds(c, 128, stride=cols), :].T
+    fext[pl.ds(HALO, rows)] = cell_f[...].astype(BF16).reshape(rows, cols, 128)
+    to_hbm = pltpu.make_async_copy(fext.at[pl.ds(HALO, rows)], cells_out, out_sem)
+    to_hbm.start()
 
     @pl.when(jnp.logical_not(early))
     def _():
         for copy in copies[2:]:
             copy.start()
-
-    work[...] = jnp.zeros(work.shape, F32)
 
     comp[...] = jnp.zeros(comp.shape, BF16)
     row_i = lax.broadcasted_iota(jnp.int32, (256, 256), 0) // HEAD_DIM
@@ -143,7 +141,7 @@
     qi = lax.broadcasted_iota(jnp.int32, (TR * cols, 1), 0)
     row_off = key_row - qi // cols
     col_off = key_col - qi % cols
-    for load in loads[2:7]:
+    for load in loads[1:6]:
         load.wait()
     near = (row_off >= 0) & (row_off <= 2 * HALO) & (col_off >= -HALO) & (col_off <= HALO)
     base = jnp.where(near, 1.0, 0.0).astype(F32)
@@ -174,7 +172,7 @@
         comp[128 : 128 + x.shape[0], at : at + x.shape[1]] = lo
 
     put(nt(enc_v, enc_v) * (1.0 / enc_v.shape[1]), 2 * hd)
-    for load, w, at in ((loads[7], wk, 0), (loads[8], wv, hd), (loads[9], wq, 2 * hd + 128)):
+    for load, w, at in ((loads[6], wk, 0), (loads[7], wv, hd), (loads[8], wq, 2 * hd + 128)):
         load.wait()
         put(nn(wg_hi, w[...]) + nn(wg_lo, w[...]), at)
 
@@ -272,15 +270,15 @@
         own_part(t, 0)
 
     lead = HALO * SIDE
-    for halo, x_ref, up_ref, down_ref, at in (
-        (halo_l, x_l, c_ul, c_dl, cols - SIDE), (halo_r, x_r, c_ur, c_dr, 0)
+    pad = jnp.zeros((128 - deep, rows), F32)
+    for halo, x_ref, up_ref, down_ref, at, slot in (
+        (halo_l, x_l, c_ul, c_dl, cols - SIDE, SIDE - HALO), (halo_r, x_r, c_ur, c_dr, 0, 0)
     ):
-        work[0 : chan * SIDE, :] = halo[...].astype(F32).reshape(chan * SIDE, rows)
         x_ref[0:lead, :] = up_ref[...].astype(F32)[:, at : at + SIDE].reshape(lead, 128)
         x_ref[lead + rows * SIDE :, :] = down_ref[...].astype(F32)[:, at : at + SIDE].reshape(lead, 128)
-        for c in range(SIDE):
-            block = work[pl.ds(c, 128, stride=SIDE), :]
-            x_ref[pl.ds(lead + c, rows, stride=SIDE), :] = block.T
+        for c in range(HALO):
+            block = jnp.concatenate([halo[c].astype(F32), pad], axis=0)
+            x_ref[pl.ds(lead + slot + c, rows, stride=SIDE), :] = block.T
 
     cside = chunk_of(ext // 2, 14) * 2 * SIDE
 
@@ -296,12 +294,13 @@
 
     for copy in copies:
         copy.wait_send()
+    to_hbm.wait()
 
 
 def out_kernel(fields, w_enc, mix, w_out, out):
     f = fields[...]
     n = f.shape[0] * f.shape[1]
-    latents = nn(f.reshape(n, f.shape[2]), w_enc[...]).astype(BF16)
+    latents = nn(f.reshape(n, f.shape[2])[:, 0 : w_enc.shape[0]], w_enc[...]).astype(BF16)
     res = latents.astype(F32) + nn(mix[...], w_out[...])
     out[...] = res.astype(BF16).reshape(out.shape)
 
@@ -312,31 +311,32 @@
     cells = rows * cols
     ext = rows + 2 * HALO
     fields_t = jnp.transpose(fields, (2, 1, 0))
+    deep = -(-chan // 16) * 16
     hbm = pl.BlockSpec(memory_space=pltpu.HBM)
     vmem = pl.BlockSpec(memory_space=pltpu.VMEM)
     keys = (TR + 2 * HALO) * (cols + 2 * SIDE)
-    mix = pl.pallas_call(
+    mix, by_cell = pl.pallas_call(
         functools.partial(attend_kernel, n_lat, n_lon, rows, cols, chan, hd),
-        out_shape=jax.ShapeDtypeStruct((cells, hd), BF16),
-        in_specs=[hbm] * 10,
-        out_specs=vmem,
+        out_shape=(jax.ShapeDtypeStruct((cells, hd), BF16), jax.ShapeDtypeStruct((rows, cols, 128), BF16)),
+        in_specs=[hbm] * 9,
+        out_specs=(vmem, hbm),
         scratch_shapes=[
             pltpu.VMEM((cells, hd), F32),
             pltpu.VMEM((cells, hd), F32),
             pltpu.VMEM((chan, cols, rows), BF16),
-            pltpu.VMEM((128 * SIDE, rows), F32),
+            pltpu.VMEM((128 * cols, rows), F32),
+            pltpu.VMEM((cells, 128), F32),
             pltpu.VMEM((ext * SIDE, 128), F32),
             pltpu.VMEM((ext * SIDE, 128), F32),
             pltpu.VMEM((HALO, cols, 128), BF16),
             pltpu.VMEM((HALO, cols, 128), BF16),
             pltpu.VMEM((HALO, cols, 128), BF16),
             pltpu.VMEM((HALO, cols, 128), BF16),
-            pltpu.VMEM((rows, cols, chan), BF16),
             pltpu.VMEM((ext, cols, 128), BF16),
-            pltpu.VMEM((chan // 2, 16, rows), BF16),
-            pltpu.VMEM((chan // 2, 16, rows), BF16),
-            pltpu.VMEM((chan // 2, 16, rows), BF16),
-            pltpu.VMEM((chan // 2, 16, rows), BF16),
+            pltpu.VMEM((HALO, deep, rows), BF16),
+            pltpu.VMEM((HALO, deep, rows), BF16),
+            pltpu.VMEM((HALO, deep, rows), BF16),
+            pltpu.VMEM((HALO, deep, rows), BF16),
             pltpu.VMEM((chan, d), BF16),
             pltpu.VMEM((1, d), F32),
             pltpu.VMEM((d, hd), BF16),
@@ -355,15 +355,16 @@
             pltpu.VMEM((ext * SIDE, hd), BF16),
             pltpu.VMEM((ext * SIDE, hd), BF16),
             pltpu.VMEM((7, TR * cols, keys), BF16),
-            pltpu.SemaphoreType.DMA((10,)),
+            pltpu.SemaphoreType.DMA((9,)),
             pltpu.SemaphoreType.DMA((8,)),
             pltpu.SemaphoreType.DMA((8,)),
+            pltpu.SemaphoreType.DMA,
         ],
         compiler_params=pltpu.CompilerParams(
             collective_id=0, has_side_effects=True, vmem_limit_bytes=63 * 1024 * 1024
         ),
     )(
-        fields, fields_t, row_valid, w_encode, norm_gain.reshape(1, d), w_query, w_key, w_value,
+        fields_t, row_valid, w_encode, norm_gain.reshape(1, d), w_query, w_key, w_value,
         query_gain.reshape(1, HEAD_DIM), key_gain.reshape(1, HEAD_DIM),
     )
     block = chunk_of(rows, 32)
@@ -372,14 +373,14 @@
         grid=(rows // block,),
         out_shape=jax.ShapeDtypeStruct((rows, cols, d), BF16),
         in_specs=[
-            pl.BlockSpec((block, cols, chan), lambda i: (i, 0, 0)),
+            pl.BlockSpec((block, cols, 128), lambda i: (i, 0, 0)),
             pl.BlockSpec((chan, d), lambda i: (0, 0)),
             pl.BlockSpec((block * cols, hd), lambda i: (i, 0)),
             pl.BlockSpec((hd, d), lambda i: (0, 0)),
         ],
         out_specs=pl.BlockSpec((block, cols, d), lambda i: (i, 0, 0)),
         compiler_params=pltpu.CompilerParams(vmem_limit_bytes=63 * 1024 * 1024),
-    )(fields, w_encode, mix, w_out)
+    )(by_cell, w_encode, mix, w_out)
 
 
 def solution(mesh):

time: 40.4 us -> 37.4 us (0.926)
  local copies, waits for them, and re-layouts: 2.29 us -> 0 us
  Pallas kernels: 37.9 us -> 37.2 us
    unnamed x1 -> x0, local copies, waits for them, and re-layouts: 2.29 us -> none
    pallas_call x1, Pallas kernels: 30.9 us -> 30.3 us  [per_device(): pl.pallas_call(functools.partial(attend_kernel, n_lat, n_lon, rows, cols,...]
where the time goes in v5:
time: 37.4 us; the launch traced here: 37.2 us
  Pallas kernels  37.2 us (99%)
    pallas_call x1, Pallas kernels, per_device(): pl.pallas_call(functools.partial(attend_kernel, n_lat, n_lon, rows, cols,...  30.3 us
    pallas_call x1, Pallas kernels, per_device(): pl.pallas_call(out_kernel, grid=(rows // block,), out_shape=jax.ShapeDtyp...  6.93 us

profile of v5, /device:TPU:1, one launch (start us, length us, event | category | flops | bytes accessed | tf_op | source)
XLA Modules:
  0.0 37.2 jit_solution(8704635930756201992)
XLA Ops:
  0.0 30.3 %shard_map.100 = (bf16[2048,512]{1,0:T(8,128)(2,1)}, bf16[128,16,128]{2,1,0:T(8,128)(2,1)}) custom-call(bf16[70,16,128]{2,1,0:T(8,128)(2,1)} %bitcast.4, s32[128]{0:T(128)} %row_valid.1, bf16[70,1024]{1,0:T(8,128)(2,1)} %w_enc.3, f32[1,1024]{1,0:T(1,128)} %bitcast.5, bf16[1024,512]{1,0:T(8,128)(2,1)} %w_q.1, bf16[1024,512]{1,0:T(8,128)(2,1)} %w_k.1, ...), custom_call_target="tpu_custom_call" | custom-call | tf_op jit(solution)/shard_map/pallas_call | solution.py:318
  30.3 6.9 %shard_map.101 = bf16[128,16,1024]{2,1,0:T(8,128)(2,1)} custom-call(bf16[128,16,128]{2,1,0:T(8,128)(2,1)} %get-tuple-element.7.fields, bf16[70,1024]{1,0:T(8,128)(2,1)} %w_enc.3, bf16[2048,512]{1,0:T(8,128)(2,1)} %get-tuple-element.8.mix, bf16[512,1024]{1,0:T(8,128)(2,1)} %w_out.1), custom_call_target="tpu_custom_call" | custom-call | tf_op jit(solution)/shard_map/pallas_call | solution.py:371

commit v6 on v5

--- a/solution.py
+++ b/solution.py
@@ -12,7 +12,9 @@
 HEAD_DIM = 64
 HALO = 6
 TR = 4
+SR = 16
 SIDE = 8
+SUNROLL = 8
 RING = 8
 EPS_ROW = 1e-05
 EPS_HEAD = 1e-06
@@ -43,7 +45,7 @@
     n_lat, n_lon, rows, cols, chan, hd,
     fields_t, row_valid, w_enc, norm_gain, w_q, w_k, w_v, query_gain, key_gain,
     mix, cells_out,
-    num_s, den_s, ft, work, cell_f, x_l, x_r, c_ul, c_ur, c_dl, c_dr, fext, send_l, send_r, halo_l, halo_r, enc, gain, wq, wk, wv, q_gain, k_gain, valid, comp, ones_blk,
+    num_l, num_r, den_l, den_r, q_l, q_r, smasks, ft, work, cell_f, x_l, x_r, c_ul, c_ur, c_dl, c_dr, fext, send_l, send_r, halo_l, halo_r, enc, gain, wq, wk, wv, q_gain, k_gain, valid, comp, ones_blk,
     q_s, k_o, v_o, k_l, v_l, k_r, v_r, masks,
     local_sem, send_sem, recv_sem, out_sem,
 ):
@@ -129,15 +131,10 @@
     col_i = lax.broadcasted_iota(jnp.int32, (256, 256), 1) // HEAD_DIM
     ones_blk[...] = jnp.where(row_i == col_i, 1.0 / HEAD_DIM, 0.0).astype(BF16)
 
-    keys = (TR + 2 * HALO) * (cols + 2 * SIDE)
     half = (TR + 2 * HALO) * cols
-    side = (TR + 2 * HALO) * SIDE
-    lane = lax.broadcasted_iota(jnp.int32, (1, keys), 1)
-    rel = jnp.where(lane < half, lane, jnp.where(lane < half + side, lane - half, lane - half - side))
-    key_row = jnp.where(lane < half, rel // cols, rel // SIDE)
-    key_col = jnp.where(
-        lane < half, rel % cols, jnp.where(lane < half + side, rel % SIDE - SIDE, rel % SIDE + cols)
-    )
+    lane = lax.broadcasted_iota(jnp.int32, (1, half), 1)
+    key_row = lane // cols
+    key_col = lane % cols
     qi = lax.broadcasted_iota(jnp.int32, (TR * cols, 1), 0)
     row_off = key_row - qi // cols
     col_off = key_col - qi % cols
@@ -147,21 +144,37 @@
     base = jnp.where(near, 1.0, 0.0).astype(F32)
     has_up = jnp.where(lat > 0, 1.0, 0.0).astype(F32)
     has_down = jnp.where(lat < n_lat - 1, 1.0, 0.0).astype(F32)
+
+    def real_rows(key_row, top, count):
+        ok = jnp.ones(key_row.shape, F32)
+        for r in range(count):
+            e = top + r
+            if e < HALO:
+                v = has_up
+            elif e >= HALO + rows:
+                v = has_down
+            else:
+                v = valid[e - HALO].astype(F32)
+            ok = jnp.where(key_row == r, v, ok)
+        return ok
+
     for slot, tile in enumerate((0, 1, 2, None, tiles - 3, tiles - 2, tiles - 1)):
-        m = base
-        if tile is not None:
-            ok = jnp.ones((1, keys), F32)
-            for r in range(TR + 2 * HALO):
-                e = tile * TR + r
-                if e < HALO:
-                    v = has_up
-                elif e >= HALO + rows:
-                    v = has_down
-                else:
-                    v = valid[e - HALO].astype(F32)
-                ok = jnp.where(key_row == r, v, ok)
-            m = base * ok
+        m = base if tile is None else base * real_rows(key_row, tile * TR, TR + 2 * HALO)
         masks[slot] = m.astype(BF16)
+
+    supers = rows // SR
+    side = 256
+    s_lane = lax.broadcasted_iota(jnp.int32, (1, side), 1)
+    s_row = s_lane // SIDE
+    si = lax.broadcasted_iota(jnp.int32, (SR * SIDE, 1), 0)
+    s_off = s_row - si // SIDE
+    for which, q_col, k_col in ((0, si % SIDE, s_lane % SIDE - SIDE), (1, si % SIDE + cols - SIDE, s_lane % SIDE + cols)):
+        c_off = k_col - q_col
+        near = (s_off >= 0) & (s_off <= 2 * HALO) & (c_off >= -HALO) & (c_off <= HALO)
+        base = jnp.where(near, 1.0, 0.0).astype(F32)
+        for slot, sup in enumerate((0, None, supers - 1)):
+            m = base if sup is None else base * real_rows(s_row, sup * SR, SR + 2 * HALO)
+            smasks[2 * slot + which] = m.astype(BF16)
 
     enc_v = enc[...]
     wg_hi, wg_lo = split(enc_v.astype(F32) * gain[...])
@@ -187,7 +200,7 @@
         sq = (x * x).astype(BF16)
         blk = ones_blk[...]
         mean = jnp.concatenate([nn(sq[:, i : i + 256], blk) for i in range(0, hd, 256)], axis=1)
-        return (x * lax.rsqrt(mean + eps_u) * g).astype(BF16)
+        return x * lax.rsqrt(mean + eps_u) * g
 
     def project(f, k_ref, v_ref, at, q_at=None):
         n = f.shape[0]
@@ -197,10 +210,15 @@
         quad = jnp.sum(y[:, 2 * hd : 2 * hd + 128] * f.astype(F32), axis=1, keepdims=True)
         u = jnp.maximum(quad, 0.0) + EPS_ROW
         eps_u = EPS_HEAD * u
-        k_ref[pl.ds(at, n), :] = head_norm(y[:, 0:hd], eps_u, kg)
+        k_ref[pl.ds(at, n), :] = head_norm(y[:, 0:hd], eps_u, kg).astype(BF16)
         v_ref[pl.ds(at, n), :] = (y[:, hd : 2 * hd] * lax.rsqrt(u)).astype(BF16)
         if q_at is not None:
-            q_s[pl.ds(q_at, n), :] = head_norm(y[:, 2 * hd + 128 :], eps_u, qg)
+            q = head_norm(y[:, 2 * hd + 128 :], eps_u, qg)
+            q_s[pl.ds(q_at, n), :] = q.astype(BF16)
+            q = q.reshape(n // cols, cols, hd)
+            h_at = pl.ds(pl.multiple_of(q_at // 2, 16), n // 2)
+            q_l[h_at, :] = q[:, 0:SIDE].reshape(n // 2, hd).astype(BF16)
+            q_r[h_at, :] = q[:, cols - SIDE :].reshape(n // 2, hd).astype(BF16)
 
     crow = chunk_of(rows, 16)
     ccell = crow * cols
@@ -219,43 +237,54 @@
             copy.start()
 
     nq = TR * cols
-    head = lax.broadcasted_iota(jnp.int32, (nq, 256), 1) // HEAD_DIM
-
-    def pick(x):
-        y = x[0:nq]
-        for h in range(1, 4):
-            y = jnp.where(head == h, x[h * nq : (h + 1) * nq], y)
-        return y
-
-    def partial(t, p, k, v, lanes):
-        ps = slice(256 * p, 256 * p + 256)
-        q_at = pl.ds(pl.multiple_of(t * nq, nq), nq)
-        slot = jnp.minimum(t, 3) + jnp.maximum(t - (tiles - 4), 0)
-        q = q_s[q_at, ps]
+    head = lax.broadcasted_iota(jnp.int32, (SR * SIDE, 256), 1) // HEAD_DIM
+
+    def partial(q, k, v, m):
+        n = q.shape[0]
+        lanes = head[0:n]
+
+        def pick(x):
+            y = x[0:n]
+            for h in range(1, 4):
+                y = jnp.where(lanes == h, x[h * n : (h + 1) * n], y)
+            return y
+
         zero = jnp.zeros_like(q)
-        q4 = jnp.concatenate([jnp.where(head == h, q, zero) for h in range(4)], axis=0)
-        m = masks[slot, :, lanes]
+        q4 = jnp.concatenate([jnp.where(lanes == h, q, zero) for h in range(4)], axis=0)
         e = jnp.exp2(nt(q4, k)).astype(BF16) * jnp.concatenate([m] * 4, axis=0)
         den = jnp.sum(e.astype(F32), axis=1, keepdims=True)
-        return q_at, ps, pick(nn(e, v)), pick(den)
+        return pick(nn(e, v)), pick(den)
 
     def own_part(t, c):
         o_at = pl.ds(pl.multiple_of(t * nq, nq), half)
+        q_at = pl.ds(pl.multiple_of(t * nq, nq), nq)
+        h_at = pl.ds(pl.multiple_of(t * (nq // 2), nq // 2), nq // 2)
+        slot = jnp.minimum(t, 3) + jnp.maximum(t - (tiles - 4), 0)
         for p in range(hd // 256):
             ps = slice(256 * p, 256 * p + 256)
-            q_at, ps, num, den = partial(t, p, k_o[o_at, ps], v_o[o_at, ps], slice(0, half))
-            num_s[q_at, ps] = num
-            den_s[q_at, ps] = den
+            num, den = partial(q_s[q_at, ps], k_o[o_at, ps], v_o[o_at, ps], masks[slot])
+            for x, left_ref, right_ref in ((num, num_l, num_r), (den, den_l, den_r)):
+                x = x.reshape(TR, cols, 256)
+                left_ref[h_at, ps] = x[:, 0:SIDE].reshape(nq // 2, 256)
+                right_ref[h_at, ps] = x[:, cols - SIDE :].reshape(nq // 2, 256)
         return c
 
-    def side_part(t, c):
-        s_at = pl.ds(pl.multiple_of(t * TR * SIDE, TR * SIDE), side)
+    def side_part(u, c):
+        ns = SR * SIDE
+        q_at = pl.ds(pl.multiple_of(u * ns, ns), ns)
+        s_at = pl.ds(pl.multiple_of(u * ns, ns), side)
+        slot = 2 * (jnp.minimum(u, 1) + jnp.maximum(u - (supers - 2), 0))
         for p in range(hd // 256):
             ps = slice(256 * p, 256 * p + 256)
-            k = jnp.concatenate([k_l[s_at, ps], k_r[s_at, ps]], axis=0)
-            v = jnp.concatenate([v_l[s_at, ps], v_r[s_at, ps]], axis=0)
-            q_at, ps, num, den = partial(t, p, k, v, slice(half, keys))
-            mix[q_at, ps] = ((num_s[q_at, ps] + num) / (den_s[q_at, ps] + den)).astype(BF16)
+            halves = []
+            for which, q_ref, k_ref, v_ref, num_ref, den_ref in (
+                (0, q_l, k_l, v_l, num_l, den_l), (1, q_r, k_r, v_r, num_r, den_r)
+            ):
+                num, den = partial(q_ref[q_at, ps], k_ref[s_at, ps], v_ref[s_at, ps], smasks[slot + which])
+                got = (num_ref[q_at, ps] + num) / (den_ref[q_at, ps] + den)
+                halves.append(got.reshape(SR, SIDE, 256))
+            both = jnp.concatenate(halves, axis=1).reshape(SR * cols, 256)
+            mix[pl.ds(pl.multiple_of(u * SR * cols, SR * cols), SR * cols), ps] = both.astype(BF16)
         return c
 
     edge = -(-HALO // TR)
@@ -275,12 +304,13 @@
         (halo_l, x_l, c_ul, c_dl, cols - SIDE, SIDE - HALO), (halo_r, x_r, c_ur, c_dr, 0, 0)
     ):
         x_ref[0:lead, :] = up_ref[...].astype(F32)[:, at : at + SIDE].reshape(lead, 128)
-        x_ref[lead + rows * SIDE :, :] = down_ref[...].astype(F32)[:, at : at + SIDE].reshape(lead, 128)
+        x_ref[lead + rows * SIDE : ext * SIDE, :] = down_ref[...].astype(F32)[:, at : at + SIDE].reshape(lead, 128)
         for c in range(HALO):
             block = jnp.concatenate([halo[c].astype(F32), pad], axis=0)
             x_ref[pl.ds(lead + slot + c, rows, stride=SIDE), :] = block.T
 
-    cside = chunk_of(ext // 2, 14) * 2 * SIDE
+    total = x_l.shape[0]
+    cside = chunk_of(total // 16, 14) * 16
 
     def side_step(i, c):
         for x_ref, k_ref, v_ref in ((x_l, k_l, v_l), (x_r, k_r, v_r)):
@@ -288,9 +318,9 @@
             project(x_ref[pl.ds(at, cside), :].astype(BF16), k_ref, v_ref, at)
         return c
 
-    lax.fori_loop(0, ext * SIDE // cside, side_step, 0, unroll=5)
-
-    lax.fori_loop(0, tiles, side_part, 0, unroll=8)
+    lax.fori_loop(0, total // cside, side_step, 0, unroll=6)
+
+    lax.fori_loop(0, supers, side_part, 0, unroll=SUNROLL)
 
     for copy in copies:
         copy.wait_send()
@@ -314,20 +344,26 @@
     deep = -(-chan // 16) * 16
     hbm = pl.BlockSpec(memory_space=pltpu.HBM)
     vmem = pl.BlockSpec(memory_space=pltpu.VMEM)
-    keys = (TR + 2 * HALO) * (cols + 2 * SIDE)
+    keys = (TR + 2 * HALO) * cols
+    side_cells = (rows - SR) * SIDE + 256
     mix, by_cell = pl.pallas_call(
         functools.partial(attend_kernel, n_lat, n_lon, rows, cols, chan, hd),
         out_shape=(jax.ShapeDtypeStruct((cells, hd), BF16), jax.ShapeDtypeStruct((rows, cols, 128), BF16)),
         in_specs=[hbm] * 9,
         out_specs=(vmem, hbm),
         scratch_shapes=[
-            pltpu.VMEM((cells, hd), F32),
-            pltpu.VMEM((cells, hd), F32),
+            pltpu.VMEM((cells // 2, hd), F32),
+            pltpu.VMEM((cells // 2, hd), F32),
+            pltpu.VMEM((cells // 2, hd), F32),
+            pltpu.VMEM((cells // 2, hd), F32),
+            pltpu.VMEM((cells // 2, hd), BF16),
+            pltpu.VMEM((cells // 2, hd), BF16),
+            pltpu.VMEM((6, SR * SIDE, 256), BF16),
             pltpu.VMEM((chan, cols, rows), BF16),
             pltpu.VMEM((128 * cols, rows), F32),
             pltpu.VMEM((cells, 128), F32),
-            pltpu.VMEM((ext * SIDE, 128), F32),
-            pltpu.VMEM((ext * SIDE, 128), F32),
+            pltpu.VMEM((side_cells, 128), F32),
+            pltpu.VMEM((side_cells, 128), F32),
             pltpu.VMEM((HALO, cols, 128), BF16),
             pltpu.VMEM((HALO, cols, 128), BF16),
             pltpu.VMEM((HALO, cols, 128), BF16),
@@ -350,10 +386,10 @@
             pltpu.VMEM((cells, hd), BF16),
             pltpu.VMEM((ext * cols, hd), BF16),
             pltpu.VMEM((ext * cols, hd), BF16),
-            pltpu.VMEM((ext * SIDE, hd), BF16),
-            pltpu.VMEM((ext * SIDE, hd), BF16),
-            pltpu.VMEM((ext * SIDE, hd), BF16),
-            pltpu.VMEM((ext * SIDE, hd), BF16),
+            pltpu.VMEM((side_cells, hd), BF16),
+            pltpu.VMEM((side_cells, hd), BF16),
+            pltpu.VMEM((side_cells, hd), BF16),
+            pltpu.VMEM((side_cells, hd), BF16),
             pltpu.VMEM((7, TR * cols, keys), BF16),
             pltpu.SemaphoreType.DMA((9,)),
             pltpu.SemaphoreType.DMA((8,)),

time: 37.4 us -> 35.7 us (0.955)
  Pallas kernels: 37.2 us -> 35.5 us
    pallas_call x1, Pallas kernels: 30.3 us -> 28.6 us  [per_device(): pl.pallas_call(functools.partial(attend_kernel, n_lat, n_lon, rows, cols,...]
where the time goes in v6:
time: 35.7 us; the launch traced here: 35.5 us
  Pallas kernels  35.5 us (99%)
    pallas_call x1, Pallas kernels, per_device(): pl.pallas_call(functools.partial(attend_kernel, n_lat, n_lon, rows, cols,...  28.6 us
    pallas_call x1, Pallas kernels, per_device(): pl.pallas_call(out_kernel, grid=(rows // block,), out_shape=jax.ShapeDtyp...  6.93 us

profile of v6, /device:TPU:1, one launch (start us, length us, event | category | flops | bytes accessed | tf_op | source)
XLA Modules:
  0.0 35.5 jit_solution(17425149422870297350)
XLA Ops:
  0.0 28.6 %shard_map.100 = (bf16[2048,512]{1,0:T(8,128)(2,1)}, bf16[128,16,128]{2,1,0:T(8,128)(2,1)}) custom-call(bf16[70,16,128]{2,1,0:T(8,128)(2,1)} %bitcast.4, s32[128]{0:T(128)} %row_valid.1, bf16[70,1024]{1,0:T(8,128)(2,1)} %w_enc.3, f32[1,1024]{1,0:T(1,128)} %bitcast.5, bf16[1024,512]{1,0:T(8,128)(2,1)} %w_q.1, bf16[1024,512]{1,0:T(8,128)(2,1)} %w_k.1, ...), custom_call_target="tpu_custom_call" | custom-call | tf_op jit(solution)/shard_map/pallas_call | solution.py:349
  28.6 6.9 %shard_map.101 = bf16[128,16,1024]{2,1,0:T(8,128)(2,1)} custom-call(bf16[128,16,128]{2,1,0:T(8,128)(2,1)} %get-tuple-element.7.fields, bf16[70,1024]{1,0:T(8,128)(2,1)} %w_enc.3, bf16[2048,512]{1,0:T(8,128)(2,1)} %get-tuple-element.8.mix, bf16[512,1024]{1,0:T(8,128)(2,1)} %w_out.1), custom_call_target="tpu_custom_call" | custom-call | tf_op jit(solution)/shard_map/pallas_call | solution.py:407

commit v7 on v6

--- a/solution.py
+++ b/solution.py
@@ -269,29 +269,34 @@
                 right_ref[h_at, ps] = x[:, cols - SIDE :].reshape(nq // 2, 256)
         return c
 
-    def side_part(u, c):
+    def side_half(u, p, which, q_ref, k_ref, v_ref, num_ref, den_ref):
         ns = SR * SIDE
+        ps = slice(256 * p, 256 * p + 256)
         q_at = pl.ds(pl.multiple_of(u * ns, ns), ns)
         s_at = pl.ds(pl.multiple_of(u * ns, ns), side)
-        slot = 2 * (jnp.minimum(u, 1) + jnp.maximum(u - (supers - 2), 0))
+        slot = 2 * (jnp.minimum(u, 1) + jnp.maximum(u - (supers - 2), 0)) + which
+        num, den = partial(q_ref[q_at, ps], k_ref[s_at, ps], v_ref[s_at, ps], smasks[slot])
+        return q_at, ps, (num_ref[q_at, ps] + num) / (den_ref[q_at, ps] + den)
+
+    def right_part(u, c):
         for p in range(hd // 256):
-            ps = slice(256 * p, 256 * p + 256)
-            halves = []
-            for which, q_ref, k_ref, v_ref, num_ref, den_ref in (
-                (0, q_l, k_l, v_l, num_l, den_l), (1, q_r, k_r, v_r, num_r, den_r)
-            ):
-                num, den = partial(q_ref[q_at, ps], k_ref[s_at, ps], v_ref[s_at, ps], smasks[slot + which])
-                got = (num_ref[q_at, ps] + num) / (den_ref[q_at, ps] + den)
-                halves.append(got.reshape(SR, SIDE, 256))
-            both = jnp.concatenate(halves, axis=1).reshape(SR * cols, 256)
+            q_at, ps, got = side_half(u, p, 1, q_r, k_r, v_r, num_r, den_r)
+            num_r[q_at, ps] = got
+        return c
+
+    def left_part(u, c):
+        for p in range(hd // 256):
+            q_at, ps, got = side_half(u, p, 0, q_l, k_l, v_l, num_l, den_l)
+            both = [x.reshape(SR, SIDE, 256) for x in (got, num_r[q_at, ps])]
+            both = jnp.concatenate(both, axis=1).reshape(SR * cols, 256)
             mix[pl.ds(pl.multiple_of(u * SR * cols, SR * cols), SR * cols), ps] = both.astype(BF16)
         return c
 
     edge = -(-HALO // TR)
     lax.fori_loop(edge, tiles - edge, own_part, 0, unroll=chunk_of(tiles - 2 * edge, 7))
 
-    for copy in copies:
-        copy.wait_recv()
+    for i in (2, 3):
+        copies[i].wait_recv()
 
     for r0 in (0, HALO + rows):
         project(fext[r0 : r0 + HALO].reshape(HALO * cols, 128), k_o, v_o, r0 * cols)
@@ -300,27 +305,27 @@
 
     lead = HALO * SIDE
     pad = jnp.zeros((128 - deep, rows), F32)
-    for halo, x_ref, up_ref, down_ref, at, slot in (
-        (halo_l, x_l, c_ul, c_dl, cols - SIDE, SIDE - HALO), (halo_r, x_r, c_ur, c_dr, 0, 0)
+    total = x_l.shape[0]
+    cside = chunk_of(total // 16, 14) * 16
+    for arrivals, halo, x_ref, k_ref, v_ref, up_ref, down_ref, at, slot, part in (
+        ((0, 4, 5), halo_r, x_r, k_r, v_r, c_ur, c_dr, 0, 0, right_part),
+        ((1, 6, 7), halo_l, x_l, k_l, v_l, c_ul, c_dl, cols - SIDE, SIDE - HALO, left_part),
     ):
+        for i in arrivals:
+            copies[i].wait_recv()
         x_ref[0:lead, :] = up_ref[...].astype(F32)[:, at : at + SIDE].reshape(lead, 128)
         x_ref[lead + rows * SIDE : ext * SIDE, :] = down_ref[...].astype(F32)[:, at : at + SIDE].reshape(lead, 128)
         for c in range(HALO):
             block = jnp.concatenate([halo[c].astype(F32), pad], axis=0)
             x_ref[pl.ds(lead + slot + c, rows, stride=SIDE), :] = block.T
 
-    total = x_l.shape[0]
-    cside = chunk_of(total // 16, 14) * 16
-
-    def side_step(i, c):
-        for x_ref, k_ref, v_ref in ((x_l, k_l, v_l), (x_r, k_r, v_r)):
+        def side_step(i, c):
             at = pl.multiple_of(i * cside, 16)
             project(x_ref[pl.ds(at, cside), :].astype(BF16), k_ref, v_ref, at)
-        return c
-
-    lax.fori_loop(0, total // cside, side_step, 0, unroll=6)
-
-    lax.fori_loop(0, supers, side_part, 0, unroll=SUNROLL)
+            return c
+
+        lax.fori_loop(0, total // cside, side_step, 0, unroll=6)
+        lax.fori_loop(0, supers, part, 0, unroll=SUNROLL)
 
     for copy in copies:
         copy.wait_send()

time: 35.7 us -> 35.6 us (level)
  no operation moved by 1% of the time
where the time goes in v7:
time: 35.6 us; the launch traced here: 35.5 us
  Pallas kernels  35.5 us (100%)
    pallas_call x1, Pallas kernels, per_device(): pl.pallas_call(functools.partial(attend_kernel, n_lat, n_lon, rows, cols,...  28.5 us
    pallas_call x1, Pallas kernels, per_device(): pl.pallas_call(out_kernel, grid=(rows // block,), out_shape=jax.ShapeDtyp...  6.93 us

profile of v7, /device:TPU:1, one launch (start us, length us, event | category | flops | bytes accessed | tf_op | source)
XLA Modules:
  0.0 35.5 jit_solution(1917736631254202476)
XLA Ops:
  0.0 28.5 %shard_map.100 = (bf16[2048,512]{1,0:T(8,128)(2,1)}, bf16[128,16,128]{2,1,0:T(8,128)(2,1)}) custom-call(bf16[70,16,128]{2,1,0:T(8,128)(2,1)} %bitcast.4, s32[128]{0:T(128)} %row_valid.1, bf16[70,1024]{1,0:T(8,128)(2,1)} %w_enc.3, f32[1,1024]{1,0:T(1,128)} %bitcast.5, bf16[1024,512]{1,0:T(8,128)(2,1)} %w_q.1, bf16[1024,512]{1,0:T(8,128)(2,1)} %w_k.1, ...), custom_call_target="tpu_custom_call" | custom-call | tf_op jit(solution)/shard_map/pallas_call | solution.py:354
  28.5 6.9 %shard_map.101 = bf16[128,16,1024]{2,1,0:T(8,128)(2,1)} custom-call(bf16[128,16,128]{2,1,0:T(8,128)(2,1)} %get-tuple-element.7.fields, bf16[70,1024]{1,0:T(8,128)(2,1)} %w_enc.3, bf16[2048,512]{1,0:T(8,128)(2,1)} %get-tuple-element.8.mix, bf16[512,1024]{1,0:T(8,128)(2,1)} %w_out.1), custom_call_target="tpu_custom_call" | custom-call | tf_op jit(solution)/shard_map/pallas_call | solution.py:412
